TPU v7x, 32 devices: a whole 2x2x4 slice. The times are simulated.
32 devices in a mesh: pix: 8 (over z, y), eb: 4 (over x, core).
Axes of the slice: x: 2, y: 2, z: 4, core: 2. Of those that a mesh axis runs over, the one named last changes fastest.
Arguments:
- abundance: float32 [8192, 1024], P('pix', 'eb'), may hold values from -60 to 60
- spectra: float32 [8192, 512], P('pix', 'eb'), may hold values from -6 to 6
- support: int32 [64, 16], P('pix', 'eb'), may hold values 0 or 1
- panel_blocks: int32 [2], replicated, may hold values from 0 to 15, as said below
Outputs:
- trailing: float32 [8192, 1024], P('pix', 'eb')
- residual: float32 [8192, 512], P('pix', 'eb')
- coefficients: float32 [2, 64, 512], P(None, None, 'eb')
Inputs may be any that keep to these rules, and one draw needn't show every extreme that they name: `panel_blocks`: the 2 entries are different column blocks, and the last column block is always among them.
All inputs are finite; a program needn't handle non-finite values. No bound on the sum of `support` on one device may be relied on, other than what follows from the above.
Results may differ from a plain program's by a relative error of at most 0.00016.
Values sent between devices are 32-bit elements; how exact they have to be, the bound alone decides.
A program may use at most 64 MiB of HBM per device.

v0:
```python
import jax
import jax.numpy as jnp
from jax import lax
from jax.sharding import PartitionSpec as P

PANEL = 64
TILE_ROWS = 128
NPANELS = 2


def broadcast(block, axis, holder):
    block = jnp.where(lax.axis_index(axis) == holder, block, jnp.zeros_like(block))
    return lax.psum(block, axis)


def product(left, right):
    return jnp.dot(left, right, precision=lax.Precision.HIGHEST)


def expand_support(abundance, support):
    row_count, col_count = abundance.shape
    support_f = support.astype(jnp.float32)
    tiled = abundance.reshape(row_count // TILE_ROWS, TILE_ROWS, col_count // PANEL, PANEL)
    return (tiled * support_f[:, None, :, None]).reshape(row_count, col_count)


def per_device(abundance, spectra, support, panel_blocks):
    matrix_x = expand_support(abundance, support)
    matrix_y = spectra
    blocks_here = matrix_x.shape[1] // PANEL
    collected = []
    for panel_index in range(NPANELS):
        block_id = panel_blocks[panel_index]
        owner_index = block_id // blocks_here
        offset = block_id % blocks_here * PANEL
        own_panel_t = lax.dynamic_slice_in_dim(matrix_x, offset, PANEL, 1).T
        gram_sum = lax.psum(product(own_panel_t, own_panel_t.T), "pix")
        factor = jnp.linalg.cholesky(gram_sum)
        local_basis = jax.scipy.linalg.solve_triangular(factor, own_panel_t, lower=True)
        shared = broadcast(local_basis, "eb", owner_index)
        proj_a, proj_b = lax.psum((product(shared, matrix_x), product(shared, matrix_y)), "pix")
        matrix_x = matrix_x - product(shared.T, proj_a)
        matrix_y = matrix_y - product(shared.T, proj_b)
        collected.append(proj_b)
    return (matrix_x, matrix_y, jnp.stack(collected))


def solution(mesh):
    placed = (P("pix", "eb"), P("pix", "eb"), P("pix", "eb"), P())
    return jax.shard_map(
        per_device,
        mesh=mesh,
        in_specs=placed,
        out_specs=(P("pix", "eb"), P("pix", "eb"), P(None, None, "eb")),
        check_vma=False,
    )
```

profile of v0, /device:TPU:0, one launch (start us, length us, event | category | flops | bytes accessed | tf_op | source)
XLA Modules:
  0.0 332.1 jit_solution(8823895906708740587)
XLA Ops:
  7.2 0.0 all-reduce.6.cloned.1.call-start
  7.2 0.6 copy-done.4
  7.8 0.6 fusion.18
  11.0 0.0 copy-start.3
  11.0 0.7 copy-done.3
  11.7 1.6 copy.7
  13.3 0.1 mul.17
  13.4 0.3 bitcast_multiply_fusion
  13.7 0.4 fusion.6
  14.1 38.9 %psum.56 = f32[64,64]{0,1:T(8,128)S(1)} all-reduce(f32[64,64]{0,1:T(8,128)S(1)} %fusion.6), channel_id=1, replica_groups=mesh['pix'=8,'eb'=4] {'pix'}, use_global_device_ids=true, to_apply=%region_0.1 | all-reduce | flops 4096 | bytes 32768 | tf_op jit(solution)/shard_map/psum | solution.py:37
  53.0 0.1 copy.9
  53.1 5.8 %cholesky.44 = f32[64,64]{1,0:T(8,128)S(1)} custom-call(f32[64,64]{1,0:T(8,128)S(1)} %fusion.13), custom_call_target="Cholesky" | custom-call | tf_op jit(solution)/shard_map/jit(cholesky)/cholesky | solution.py:38
  58.9 0.6 compare_reduce_fusion.1
  59.6 0.7 fusion.8
  60.2 4.9 %custom-call.6 = f32[1,64,64]{1,2,0:T(8,128)S(1)} custom-call(f32[1,64,64]{2,1,0:T(8,128)S(1)} %fusion.8), custom_call_target="InvertDiagBlocksLowerTriangular" | custom-call | tf_op jit(solution)/shard_map/jit(_solve_triangular)/triangular_solve | solution.py:39
  65.2 1.1 convolution_select_fusion.1
  66.3 0.0 all-reduce.6.cloned.1.call-update
  66.3 0.0 all-reduce.8.cloned.1.call-start
  69.0 0.0 copy-start.2
  69.0 26.7 %all-reduce.6.cloned.1.call-done = f32[64,1024]{1,0:T(8,128)} async-done(((f32[64,1024]{1,0:T(8,128)}), f32[64,1024]{1,0:T(8,128)}) %all-reduce.6.cloned.1.call-update) | async-done | bytes 262160 | tf_op jit(solution)/shard_map/psum | solution.py:13
  95.7 2.7 fusion.19
  98.4 0.0 all-reduce.8.cloned.1.call-update
  98.5 0.0 all-reduce.10.cloned.1.call-start
  98.5 0.0 copy-done.2
  98.5 0.4 fusion.21
  99.0 69.6 %all-reduce.8.cloned.1.call-done = f32[64,256]{1,0:T(8,128)} async-done(((f32[64,256]{1,0:T(8,128)}), f32[64,256]{1,0:T(8,128)}) %all-reduce.8.cloned.1.call-update) | async-done | bytes 65552 | tf_op jit(solution)/shard_map/psum | solution.py:41
  168.5 1.9 convolution_subtract_fusion.1
  170.4 0.4 fusion.3
  170.8 36.6 %all-reduce = (f32[64,64]{0,1:T(8,128)S(1)}, f32[64,128]{1,0:T(8,128)S(1)}) all-reduce(f32[64,64]{0,1:T(8,128)S(1)} %fusion.3, f32[64,128]{1,0:T(8,128)S(1)} %fusion.21), channel_id=1, replica_groups=mesh['pix'=8,'eb'=4] {'pix'}, use_global_device_ids=true, to_apply=%region_5.8 | all-reduce | flops 12288 | bytes 98304 | tf_op jit(solution)/shard_map/psum | solution.py:37
  207.3 0.1 copy.11
  207.4 5.8 %cholesky.55 = f32[64,64]{1,0:T(8,128)S(1)} custom-call(f32[64,64]{1,0:T(8,128)S(1)} %fusion.11), custom_call_target="Cholesky" | custom-call | tf_op jit(solution)/shard_map/jit(cholesky)/cholesky | solution.py:38
  213.3 0.6 compare_reduce_fusion
  214.0 0.7 fusion.9
  214.6 4.9 %custom-call.7 = f32[1,64,64]{1,2,0:T(8,128)S(1)} custom-call(f32[1,64,64]{2,1,0:T(8,128)S(1)} %fusion.9), custom_call_target="InvertDiagBlocksLowerTriangular" | custom-call | tf_op jit(solution)/shard_map/jit(_solve_triangular)/triangular_solve | solution.py:39
  219.5 1.1 convolution_select_fusion
  220.7 0.0 all-reduce.10.cloned.1.call-update
  220.7 0.0 all-reduce.12.cloned.1.call-start
  220.7 1.0 convolution_subtract_fusion.3
  221.7 28.3 %all-reduce.10.cloned.1.call-done = f32[64,1024]{1,0:T(8,128)} async-done(((f32[64,1024]{1,0:T(8,128)}), f32[64,1024]{1,0:T(8,128)}) %all-reduce.10.cloned.1.call-update) | async-done | bytes 262160 | tf_op jit(solution)/shard_map/psum | solution.py:13
  250.0 2.7 fusion.20
  252.8 0.0 all-reduce.12.cloned.1.call-update
  252.8 0.4 fusion.22
  253.3 37.2 %psum.63 = f32[64,128]{1,0:T(8,128)S(1)} all-reduce(f32[64,128]{1,0:T(8,128)S(1)} %fusion.22), channel_id=1, replica_groups=mesh['pix'=8,'eb'=4] {'pix'}, use_global_device_ids=true, to_apply=%region_9.12 | all-reduce | flops 8192 | bytes 65536 | tf_op jit(solution)/shard_map/psum | solution.py:41
  290.4 1.8 convolution_subtract_fusion.2
  292.2 0.6 pad_maximum_fusion
  292.8 29.6 %all-reduce.12.cloned.1.call-done = f32[64,256]{1,0:T(8,128)} async-done(((f32[64,256]{1,0:T(8,128)}), f32[64,256]{1,0:T(8,128)}) %all-reduce.12.cloned.1.call-update) | async-done | bytes 65552 | tf_op jit(solution)/shard_map/psum | solution.py:41
  322.4 1.9 convolution_subtract_fusion
  324.3 1.3 copy.13
  (10 shorter events, 0.1 us)
Async XLA Ops:
  7.2 0.7 copy-start.4
  7.2 88.5 %all-reduce.6.cloned.1.call-start = ((), (), s32[]{:S(2)}) async-start(), calls=%async_computation | async-start | bytes 524288 | tf_op jit(solution)/shard_map/psum | solution.py:13
  11.0 0.7 copy-start.3
  66.3 102.2 %all-reduce.8.cloned.1.call-start = ((), (), s32[]{:S(2)}) async-start(), calls=%async_computation.1 | async-start | bytes 131072 | tf_op jit(solution)/shard_map/psum | solution.py:41
  69.0 29.5 %copy-start.2 = (f32[1024,128]{1,0:T(8,128)S(1)}, f32[1024,128]{1,0:T(8,128)}, u32[]{:S(2)}) copy-start(f32[1024,128]{1,0:T(8,128)} %param.8) | copy-start | bytes 1572868
  95.7 2.8 copy-start
  98.5 151.6 %all-reduce.10.cloned.1.call-start = ((), (), s32[]{:S(2)}) async-start(), calls=%async_computation.2 | async-start | bytes 524288 | tf_op jit(solution)/shard_map/psum | solution.py:13
  220.7 101.7 %all-reduce.12.cloned.1.call-start = ((), (), s32[]{:S(2)}) async-start(), calls=%async_computation.3 | async-start | bytes 131072 | tf_op jit(solution)/shard_map/psum | solution.py:41
  250.0 2.8 copy-start.1
Sparse Core Ops, SparseCore 0:
  66.4 29.2 all-reduce.5
  100.1 68.4 all-reduce.7
  220.8 29.1 all-reduce.9
  253.9 68.4 all-reduce.11
where the time goes:
time: 333 us; the launch traced here: 332 us
  waiting for transfers between devices  154 us (46%)
  blocking collectives  113 us (34%)
  other arithmetic  25.1 us (8%)
  between operations  19.2 us (6%)
  matrix products  15.8 us (5%)
  local copies, waits for them, and re-layouts  5.01 us (2%)
    psum x2, waiting for transfers between devices, per_device(): lax.psum((product(shared, matrix_x), product(shared, matrix_y)), 'pix')  99.1 us
    psum x2, blocking collectives, per_device(): gram_sum = lax.psum(product(own_panel_t, own_panel_t.T), 'pix')  75.4 us
    psum x2, waiting for transfers between devices, broadcast(): return lax.psum(block, axis)  55 us
    psum x1, blocking collectives, per_device(): lax.psum((product(shared, matrix_x), product(shared, matrix_y)), 'pix')  37.2 us
    dot_general x10, matrix products, product(): return jnp.dot(left, right, precision=lax.Precision.HIGHEST)  13.6 us
    another operation x6, other arithmetic, per_device(): factor = jnp.linalg.cholesky(gram_sum)  13 us
    another operation x4, other arithmetic, per_device(): jax.scipy.linalg.solve_triangular(factor, own_panel_t, lower=True)  11.1 us
  transfers between devices with their start and end apart: 4, of which 4 were waited for; matrix products, arithmetic and copies ran while one was open for 1% of the time, Pallas kernels for 0%

commit v1 on v0

v1 whole, which is shorter than its diff:
```python
import functools

import jax
import jax.numpy as jnp
from jax import lax
from jax.experimental import pallas as pl
from jax.experimental.pallas import tpu as pltpu
from jax.sharding import PartitionSpec as P

PANEL = 64
TILE_ROWS = 128
NPANELS = 2
WIDTH = PANEL * NPANELS
SUB = 8
VMEM_LIMIT = 48 * 1024 * 1024


def product(left, right):
    return jnp.dot(left, right, precision=lax.Precision.HIGHEST, preferred_element_type=jnp.float32)


def product_t(left, right):
    return lax.dot_general(
        left,
        right,
        (((0,), (0,)), ((), ())),
        precision=lax.Precision.HIGHEST,
        preferred_element_type=jnp.float32,
    )


def support_row(support_ref, tile, cols):
    lane = lax.broadcasted_iota(jnp.int32, (1, cols), 1)
    row = jnp.zeros((1, cols), jnp.float32)
    for block in range(cols // PANEL):
        value = support_ref[tile, block].astype(jnp.float32)
        row = jnp.where((lane >= block * PANEL) & (lane < (block + 1) * PANEL), value, row)
    return row


def inverse_factor(work_ref):
    shape = (SUB, WIDTH)
    sublane = lax.broadcasted_iota(jnp.int32, shape, 0)
    for block in range(WIDTH // SUB):
        low = block * SUB
        rows_g = work_ref[low : low + SUB, :WIDTH]
        rows_t = work_ref[low : low + SUB, WIDTH:]
        columns = [jnp.broadcast_to(rows_g[:, low + j : low + j + 1], shape) for j in range(SUB)]
        entry = {
            (i, j): jnp.broadcast_to(columns[j][i : i + 1, :], shape)
            for j in range(SUB)
            for i in range(j, SUB)
        }
        g = [jnp.broadcast_to(rows_g[i : i + 1, :], shape) for i in range(SUB)]
        t = [jnp.broadcast_to(rows_t[i : i + 1, :], shape) for i in range(SUB)]
        upper = rows_g
        basis = rows_t
        for j in range(SUB):
            scale = lax.rsqrt(entry[j, j])
            for i in range(j + 1, SUB):
                entry[i, j] = entry[i, j] * scale
            g[j] = g[j] * scale
            t[j] = t[j] * scale
            for i in range(j + 1, SUB):
                for k in range(j + 1, i + 1):
                    entry[i, k] = entry[i, k] - entry[i, j] * entry[k, j]
                g[i] = g[i] - entry[i, j] * g[j]
                t[i] = t[i] - entry[i, j] * t[j]
            upper = jnp.where(sublane == j, g[j], upper)
            basis = jnp.where(sublane == j, t[j], basis)
        work_ref[low : low + SUB, WIDTH:] = basis
        if low + SUB < WIDTH:
            both = jnp.concatenate([upper, basis], axis=1)
            below = upper.T[low + SUB :, :]
            work_ref[low + SUB :, :] = work_ref[low + SUB :, :] - product(below, both)
    return work_ref[:, WIDTH:]


def gram_kernel(x_ref, y_ref, support_ref, c_ref, out_ref):
    rows, cols = x_ref.shape
    total = None
    for tile in range(rows // TILE_ROWS):
        span = pl.ds(tile * TILE_ROWS, TILE_ROWS)
        masked = x_ref[span, :] * support_row(support_ref, tile, cols)
        panel = c_ref[span, :]
        joined = jnp.concatenate([masked, y_ref[span, :], panel], axis=1)
        part = product_t(panel, joined)
        total = part if total is None else total + part
    out_ref[...] = total


def update_kernel(x_ref, y_ref, support_ref, c_ref, m_ref, trail_ref, resid_ref, coef_ref, work_ref):
    rows, cols = x_ref.shape
    bands = y_ref.shape[1]
    row = lax.broadcasted_iota(jnp.int32, (WIDTH, WIDTH), 0)
    col = lax.broadcasted_iota(jnp.int32, (WIDTH, WIDTH), 1)
    work_ref[:, :WIDTH] = m_ref[:, cols + bands :]
    work_ref[:, WIDTH:] = jnp.where(row == col, 1.0, 0.0).astype(jnp.float32)
    inverse = inverse_factor(work_ref)
    proj = product(inverse, m_ref[:, : cols + bands])
    coef_ref[...] = proj[:, cols:]
    weights = product_t(inverse, proj)
    for tile in range(rows // TILE_ROWS):
        span = pl.ds(tile * TILE_ROWS, TILE_ROWS)
        masked = x_ref[span, :] * support_row(support_ref, tile, cols)
        change = product(c_ref[span, :], weights)
        trail_ref[span, :] = masked - change[:, :cols]
        resid_ref[span, :] = y_ref[span, :] - change[:, cols:]


VMEM = pl.BlockSpec(memory_space=pltpu.VMEM)
SMEM = pl.BlockSpec(memory_space=pltpu.SMEM)


def own_panels(abundance, support, panel_blocks, holder):
    blocks_here = abundance.shape[1] // PANEL
    parts = []
    for index in range(NPANELS):
        block = panel_blocks[index]
        local = block % blocks_here
        panel = lax.dynamic_slice_in_dim(abundance, local * PANEL, PANEL, 1)
        keep = lax.dynamic_slice_in_dim(support, local, 1, 1).astype(jnp.float32)
        keep = jnp.where(block // blocks_here == holder, keep, 0.0)
        parts.append((panel.reshape(-1, TILE_ROWS, PANEL) * keep[:, :, None]).reshape(-1, PANEL))
    return jnp.concatenate(parts, axis=1)


def per_device(abundance, spectra, support, panel_blocks):
    rows, cols = abundance.shape
    bands = spectra.shape[1]
    own = own_panels(abundance, support, panel_blocks, lax.axis_index("eb"))
    panels = lax.psum(own, "eb")
    params = pltpu.CompilerParams(vmem_limit_bytes=VMEM_LIMIT)
    grams = pl.pallas_call(
        gram_kernel,
        out_shape=jax.ShapeDtypeStruct((WIDTH, cols + bands + WIDTH), jnp.float32),
        in_specs=[VMEM, VMEM, SMEM, VMEM],
        out_specs=VMEM,
        compiler_params=params,
        name="gram",
    )(abundance, spectra, support, panels)
    grams = lax.psum(grams, "pix")
    trailing, residual, coefficients = pl.pallas_call(
        update_kernel,
        out_shape=(
            jax.ShapeDtypeStruct((rows, cols), jnp.float32),
            jax.ShapeDtypeStruct((rows, bands), jnp.float32),
            jax.ShapeDtypeStruct((WIDTH, bands), jnp.float32),
        ),
        in_specs=[VMEM, VMEM, SMEM, VMEM, VMEM],
        out_specs=(VMEM, VMEM, VMEM),
        scratch_shapes=[pltpu.VMEM((WIDTH, 2 * WIDTH), jnp.float32)],
        compiler_params=params,
        name="update",
    )(abundance, spectra, support, panels, grams)
    return trailing, residual, coefficients.reshape(NPANELS, PANEL, bands)


def solution(mesh):
    placed = (P("pix", "eb"), P("pix", "eb"), P("pix", "eb"), P())
    return jax.shard_map(
        per_device,
        mesh=mesh,
        in_specs=placed,
        out_specs=(P("pix", "eb"), P("pix", "eb"), P(None, None, "eb")),
        check_vma=False,
    )
```

time: 333 us -> 148 us (0.44)
  blocking collectives: 113 us -> 0 us
  waiting for transfers between devices: 154 us -> 107 us
  other arithmetic: 25.1 us -> 2.81 us
  matrix products: 15.8 us -> 0 us
  Pallas kernels: 0 us -> 14.4 us
    psum x3 -> x0, blocking collectives: 113 us -> none  [the longest x2 75.4 us: per_device(): gram_sum = lax.psum(product(own_panel_t, own_panel_t.T), 'pix')]
    psum x4 -> x2, waiting for transfers between devices: 154 us -> 107 us  [the longest x1 70.7 us: per_device(): grams = lax.psum(grams, 'pix')]
    another operation x11 -> x0, other arithmetic: 24.8 us -> none  [the longest x6 13 us: per_device(): factor = jnp.linalg.cholesky(gram_sum)]
    pallas_call x0 -> x2, Pallas kernels: none -> 14.4 us  [the longest x1 11.3 us: per_device(): pl.pallas_call(update_kernel, out_shape=(jax.ShapeDtypeStruct((rows, cols...]
    dot_general x10 -> x0, matrix products: 13.6 us -> none  [product(): return jnp.dot(left, right, precision=lax.Precision.HIGHEST)]
  transfers between devices with their start and end apart: 4 -> 2, of which waited for: 4 -> 2; matrix products, arithmetic and copies ran while one was open for 1% -> 0% of each run, Pallas kernels for 0% -> 0%
where the time goes in v1:
time: 148 us; the launch traced here: 147 us
  waiting for transfers between devices  107 us (72%)
  between operations  19.3 us (13%)
  Pallas kernels  14.4 us (10%)
  local copies, waits for them, and re-layouts  4.01 us (3%)
  other arithmetic  2.81 us (2%)
    psum x1, waiting for transfers between devices, per_device(): grams = lax.psum(grams, 'pix')  70.7 us
    psum x1, waiting for transfers between devices, per_device(): panels = lax.psum(own, 'eb')  35.9 us
    pallas_call x1, Pallas kernels, per_device(): pl.pallas_call(update_kernel, out_shape=(jax.ShapeDtypeStruct((rows, cols...  11.3 us
    unnamed x15, local copies, waits for them, and re-layouts  3.36 us
    pallas_call x1, Pallas kernels, per_device(): pl.pallas_call(gram_kernel, out_shape=jax.ShapeDtypeStruct((WIDTH, cols +...  3.15 us
  transfers between devices with their start and end apart: 2, of which 2 were waited for; matrix products, arithmetic and copies ran while one was open for 0% of the time, Pallas kernels for 0%

profile of v1, /device:TPU:0, one launch (start us, length us, event | category | flops | bytes accessed | tf_op | source)
XLA Modules:
  0.0 147.3 jit_solution(11052723641218343315)
XLA Ops:
  7.2 0.0 copy-start.6
  7.2 0.0 all-reduce.3.cloned.1.call-start
  7.2 0.6 copy-done.6
  7.8 0.6 fusion.4
  13.6 0.0 copy-start.5
  13.7 0.7 copy-done.5
  14.3 0.1 broadcast_bitcast_fusion
  14.4 1.8 %dynamic-slice_multiply_fusion.1 = (f32[1024,64]{1,0:T(8,128)S(1)}, f32[1024,64]{1,0:T(8,128)S(1)}) fusion(f32[1024,256]{1,0:T(8,128)} %x_ref.3, s32[]{:T(128)S(6)} %select_n.45, f32[1024]{0:T(1024)S(1)} %get-tuple-element.16, f32[1024]{0:T(1024)S(1)} %get-tuple-element.15, s32[]{:T(128)S(6)} %select_n.51), kind=kLoop, calls=%fused_computation.2 | loop fusion | flops 131072 | bytes 1056776 | tf_op jit(solution)/shard_map/mul | solution.py:124
  16.2 0.0 copy-start
  16.2 1.0 pad_maximum_fusion
  17.2 0.0 copy-start.1
  17.2 0.0 all-reduce.3.cloned.1.call-update
  17.3 0.0 all-reduce.5.cloned.1.call-start
  17.3 0.1 copy.8.support_ref
  17.4 35.9 %all-reduce.3.cloned.1.call-done.c_ref = f32[1024,128]{1,0:T(8,128)} async-done(((f32[1024,128]{1,0:T(8,128)}), f32[1024,128]{1,0:T(8,128)}) %all-reduce.3.cloned.1.call-update) | async-done | bytes 524304 | tf_op jit(solution)/shard_map/psum | solution.py:132
  53.3 0.0 copy-done
  53.3 0.0 copy-done.1
  53.3 0.0 copy-start.2
  53.3 1.0 copy-done.2
  54.4 0.0 copy-start.3
  54.4 3.1 %gram.1 = f32[128,512]{1,0:T(8,128)} custom-call(f32[1024,256]{1,0:T(8,128)S(1)} %copy-done, f32[1024,128]{1,0:T(8,128)S(1)} %copy-done.1, s32[8,4]{1,0:T(8,128)S(1)} %copy.8.support_ref, f32[1024,128]{1,0:T(8,128)S(1)} %copy-done.2), custom_call_target="tpu_custom_call" | custom-call | tf_op jit(solution)/shard_map/gram/pallas_call | solution.py:134
  57.5 0.0 all-reduce.5.cloned.1.call-update
  57.5 70.7 %all-reduce.5.cloned.1.call-done.m_ref = f32[128,512]{1,0:T(8,128)} async-done(((f32[128,512]{1,0:T(8,128)}), f32[128,512]{1,0:T(8,128)}) %all-reduce.5.cloned.1.call-update) | async-done | bytes 262160 | tf_op jit(solution)/shard_map/psum | solution.py:142
  128.2 0.0 copy-done.3
  128.2 0.0 copy-start.4
  128.2 0.9 copy-done.4
  129.2 11.3 %update.1 = (f32[1024,256]{1,0:T(8,128)}, f32[1024,128]{1,0:T(8,128)}, f32[128,128]{1,0:T(8,128)}) custom-call(f32[1024,256]{1,0:T(8,128)S(1)} %copy-done, f32[1024,128]{1,0:T(8,128)S(1)} %copy-done.1, s32[8,4]{1,0:T(8,128)S(1)} %copy.8.support_ref, f32[1024,128]{1,0:T(8,128)S(1)} %copy-done.3, f32[128,512]{1,0:T(8,128)S(1)} %copy-done.4), custom_call_target="tpu_custom_call" | custom-call | tf_op jit(solution)/shard_map/update/pallas_call | solution.py:143
  (1 shorter events, 0.0 us)
Async XLA Ops:
  7.2 0.7 copy-start.6
  7.2 46.1 %all-reduce.3.cloned.1.call-start = ((), (), s32[]{:S(2)}) async-start(), calls=%async_computation | async-start | bytes 1048576 | tf_op jit(solution)/shard_map/psum | solution.py:132
  13.6 0.7 copy-start.5
  16.2 37.1 %copy-start = (f32[1024,256]{1,0:T(8,128)S(1)}, f32[1024,256]{1,0:T(8,128)}, u32[]{:S(2)}) copy-start(f32[1024,256]{1,0:T(8,128)} %x_ref.3) | copy-start | bytes 3145732
  17.2 36.1 %copy-start.1 = (f32[1024,128]{1,0:T(8,128)S(1)}, f32[1024,128]{1,0:T(8,128)}, u32[]{:S(2)}) copy-start(f32[1024,128]{1,0:T(8,128)} %y_ref.3) | copy-start | bytes 1572868
  17.3 111.0 %all-reduce.5.cloned.1.call-start = ((), (), s32[]{:S(2)}) async-start(), calls=%async_computation.1 | async-start | bytes 524288 | tf_op jit(solution)/shard_map/psum | solution.py:142
  53.3 1.0 copy-start.2
  54.4 73.9 %copy-start.3 = (f32[1024,128]{1,0:T(8,128)S(1)}, f32[1024,128]{1,0:T(8,128)}, u32[]{:S(2)}) copy-start(f32[1024,128]{1,0:T(8,128)} %all-reduce.3.cloned.1.call-done.c_ref) | copy-start | bytes 1572868
  128.2 1.0 copy-start.4
Sparse Core Ops, SparseCore 0:
  17.4 35.8 all-reduce.2
  57.6 70.5 all-reduce.4

commit v2 on v1

--- a/solution.py
+++ b/solution.py
@@ -108,6 +108,184 @@
         resid_ref[span, :] = y_ref[span, :] - change[:, cols:]
 
 
+def masked_tile(x_ref, support_ref, tile):
+    span = pl.ds(pl.multiple_of(tile * TILE_ROWS, TILE_ROWS), TILE_ROWS)
+    return x_ref[span, :] * support_row(support_ref, tile, x_ref.shape[1])
+
+
+def own_panel_tile(x_ref, support_ref, blocks_ref, holder, tile):
+    cols = x_ref.shape[1]
+    blocks_here = cols // PANEL
+    span = pl.ds(pl.multiple_of(tile * TILE_ROWS, TILE_ROWS), TILE_ROWS)
+    left = lax.broadcasted_iota(jnp.int32, (1, WIDTH), 1) < PANEL
+    total = jnp.zeros((TILE_ROWS, WIDTH), jnp.float32)
+    for pair in range(cols // WIDTH):
+        values = x_ref[span, pair * WIDTH : (pair + 1) * WIDTH]
+        turned = pltpu.roll(values, PANEL, 1)
+        factors = []
+        for half in range(2):
+            local = pair * 2 + half
+            keep = support_ref[tile, local].astype(jnp.float32)
+            factors.append(
+                [jnp.where(blocks_ref[i] == holder * blocks_here + local, keep, 0.0) for i in range(2)]
+            )
+        straight = jnp.where(left, factors[0][0], factors[1][1])
+        crossed = jnp.where(left, factors[1][0], factors[0][1])
+        total = total + values * straight + turned * crossed
+    return total
+
+
+def exchange_kernel(
+    pix_count,
+    x_ref,
+    y_ref,
+    support_ref,
+    blocks_ref,
+    c_ref,
+    m_ref,
+    own,
+    first_in,
+    chip_sum,
+    second_in,
+    acc,
+    slots,
+    send1,
+    recv1,
+    send2,
+    recv2,
+    send3,
+    recv3,
+    send4,
+    recv4,
+    send5,
+    recv5,
+):
+    rows, cols = x_ref.shape
+    half = rows // 2
+    chunks = half // TILE_ROWS
+    pix = lax.axis_index("pix")
+    eb = lax.axis_index("eb")
+    core = eb % 2
+    beside = eb + 1 - 2 * core
+    across = (eb + 2) % 4
+    others = [(pix + d) % pix_count for d in range(1, pix_count)]
+
+    barrier = pltpu.get_barrier_semaphore()
+    for target in [(pix, beside), (pix, across)] + [(other, eb) for other in others]:
+        pl.semaphore_signal(barrier, inc=1, device_id=target, device_id_type=pl.DeviceIdType.MESH)
+
+    def send(src, dst, send_sem, recv_sem, target):
+        copy = pltpu.make_async_remote_copy(
+            src_ref=src,
+            dst_ref=dst,
+            send_sem=send_sem,
+            recv_sem=recv_sem,
+            device_id=target,
+            device_id_type=pl.DeviceIdType.MESH,
+        )
+        copy.start()
+        return copy
+
+    def span(side, chunk):
+        start = pl.multiple_of((side * chunks + chunk) * TILE_ROWS, TILE_ROWS)
+        return pl.ds(start, TILE_ROWS)
+
+    def piece(chunk):
+        return pl.ds(chunk * TILE_ROWS, TILE_ROWS)
+
+    def prepare(side, chunk):
+        tile = side * chunks + chunk
+        own[span(side, chunk), :] = own_panel_tile(x_ref, support_ref, blocks_ref, eb, tile)
+
+    def accumulate(side, chunk, first):
+        panel = c_ref[span(side, chunk), :]
+        masked = masked_tile(x_ref, support_ref, side * chunks + chunk)
+        joined = jnp.concatenate([masked, y_ref[span(side, chunk), :], panel], axis=1)
+        part = product_t(panel, joined)
+        if first:
+            acc[...] = part
+        else:
+            acc[...] += part
+
+    other_core = 1 - core
+    prepare(other_core, 0)
+    pl.semaphore_wait(barrier, pix_count + 1)
+    copies1 = []
+    for chunk in range(chunks):
+        if chunk > 0:
+            prepare(other_core, chunk)
+        copies1.append(
+            send(
+                own.at[span(other_core, chunk), :],
+                first_in.at[piece(chunk), :],
+                send1.at[chunk],
+                recv1.at[chunk],
+                (pix, beside),
+            )
+        )
+    for chunk in range(chunks):
+        prepare(core, chunk)
+
+    copies2 = []
+    for chunk in range(chunks):
+        copies1[chunk].wait_recv()
+        chip_sum[piece(chunk), :] = own[span(core, chunk), :] + first_in[piece(chunk), :]
+        copies2.append(
+            send(
+                chip_sum.at[piece(chunk), :],
+                second_in.at[piece(chunk), :],
+                send2.at[chunk],
+                recv2.at[chunk],
+                (pix, across),
+            )
+        )
+
+    copies3 = []
+    for chunk in range(chunks):
+        copies2[chunk].wait_recv()
+        c_ref[span(core, chunk), :] = chip_sum[piece(chunk), :] + second_in[piece(chunk), :]
+        copies3.append(
+            send(
+                c_ref.at[span(core, chunk), :],
+                c_ref.at[span(core, chunk), :],
+                send3.at[chunk],
+                recv3.at[chunk],
+                (pix, beside),
+            )
+        )
+        accumulate(core, chunk, chunk == 0)
+        if chunk > 0:
+            copies3[chunk - 1].wait_recv()
+            accumulate(other_core, chunk - 1, False)
+    copies3[chunks - 1].wait_recv()
+    accumulate(other_core, chunks - 1, False)
+
+    share = WIDTH // pix_count
+
+    def rows_of(index):
+        return pl.ds(pl.multiple_of(index * share, share), share)
+
+    copies4 = []
+    for index, other in enumerate(others):
+        copies4.append(
+            send(acc.at[rows_of(other), :], slots.at[index], send4.at[index], recv4.at[index], (other, eb))
+        )
+    total = acc[rows_of(pix), :]
+    for index in range(pix_count - 1):
+        copies4[index].wait_recv()
+        total = total + slots[index]
+    m_ref[rows_of(pix), :] = total
+    copies5 = []
+    for index, other in enumerate(others):
+        copies5.append(
+            send(m_ref.at[rows_of(pix), :], m_ref.at[rows_of(pix), :], send5.at[index], recv5.at[index], (other, eb))
+        )
+    for copy in copies5:
+        copy.wait_recv()
+    for copy in copies1 + copies2 + copies3 + copies4 + copies5:
+        copy.wait_send()
+
+
 VMEM = pl.BlockSpec(memory_space=pltpu.VMEM)
 SMEM = pl.BlockSpec(memory_space=pltpu.SMEM)
 
@@ -125,21 +303,64 @@
     return jnp.concatenate(parts, axis=1)
 
 
-def per_device(abundance, spectra, support, panel_blocks):
-    rows, cols = abundance.shape
+def sums_by_collectives(abundance, spectra, support, panel_blocks):
+    cols = abundance.shape[1]
     bands = spectra.shape[1]
     own = own_panels(abundance, support, panel_blocks, lax.axis_index("eb"))
     panels = lax.psum(own, "eb")
-    params = pltpu.CompilerParams(vmem_limit_bytes=VMEM_LIMIT)
     grams = pl.pallas_call(
         gram_kernel,
         out_shape=jax.ShapeDtypeStruct((WIDTH, cols + bands + WIDTH), jnp.float32),
         in_specs=[VMEM, VMEM, SMEM, VMEM],
         out_specs=VMEM,
-        compiler_params=params,
+        compiler_params=pltpu.CompilerParams(vmem_limit_bytes=VMEM_LIMIT),
         name="gram",
     )(abundance, spectra, support, panels)
-    grams = lax.psum(grams, "pix")
+    return panels, lax.psum(grams, "pix")
+
+
+def sums_by_copies(pix_count, abundance, spectra, support, panel_blocks):
+    rows, cols = abundance.shape
+    width = cols + spectra.shape[1] + WIDTH
+    half = rows // 2
+    chunks = half // TILE_ROWS
+    dma = pltpu.SemaphoreType.DMA
+    near = [dma((chunks,))] * 6
+    far = [dma((pix_count - 1,))] * 4
+    return pl.pallas_call(
+        functools.partial(exchange_kernel, pix_count),
+        out_shape=(
+            jax.ShapeDtypeStruct((rows, WIDTH), jnp.float32),
+            jax.ShapeDtypeStruct((WIDTH, width), jnp.float32),
+        ),
+        in_specs=[VMEM, VMEM, SMEM, SMEM],
+        out_specs=(VMEM, VMEM),
+        scratch_shapes=[
+            pltpu.VMEM((rows, WIDTH), jnp.float32),
+            pltpu.VMEM((half, WIDTH), jnp.float32),
+            pltpu.VMEM((half, WIDTH), jnp.float32),
+            pltpu.VMEM((half, WIDTH), jnp.float32),
+            pltpu.VMEM((WIDTH, width), jnp.float32),
+            pltpu.VMEM((pix_count - 1, WIDTH // pix_count, width), jnp.float32),
+        ]
+        + near
+        + far,
+        compiler_params=pltpu.CompilerParams(
+            collective_id=0, has_side_effects=True, vmem_limit_bytes=VMEM_LIMIT
+        ),
+        name="exchange",
+    )(abundance, spectra, support, panel_blocks)
+
+
+def per_device(pix_count, eb_count, abundance, spectra, support, panel_blocks):
+    rows, cols = abundance.shape
+    bands = spectra.shape[1]
+    args = (abundance, spectra, support, panel_blocks)
+    if eb_count == 4 and 1 < pix_count and WIDTH % (SUB * pix_count) == 0:
+        panels, grams = sums_by_copies(pix_count, *args)
+    else:
+        panels, grams = sums_by_collectives(*args)
+    params = pltpu.CompilerParams(vmem_limit_bytes=VMEM_LIMIT)
     trailing, residual, coefficients = pl.pallas_call(
         update_kernel,
         out_shape=(
@@ -159,7 +380,7 @@
 def solution(mesh):
     placed = (P("pix", "eb"), P("pix", "eb"), P("pix", "eb"), P())
     return jax.shard_map(
-        per_device,
+        functools.partial(per_device, mesh.shape["pix"], mesh.shape["eb"]),
         mesh=mesh,
         in_specs=placed,
         out_specs=(P("pix", "eb"), P("pix", "eb"), P(None, None, "eb")),

time: 148 us -> 45.8 us (0.31)
  waiting for transfers between devices: 107 us -> 0 us
  Pallas kernels: 14.4 us -> 41.9 us
  between operations: 19.3 us -> 0.65 us
  other arithmetic: 2.81 us -> 0 us
    psum x2 -> x0, waiting for transfers between devices: 107 us -> none  [the longest x1 70.7 us: per_device(): grams = lax.psum(grams, 'pix')]
    pallas_call x1, Pallas kernels: 3.15 us -> 30.6 us  [sums_by_copies(): pl.pallas_call(functools.partial(exchange_kernel, pix_count), out_shape=(...]
    mul x2 -> x0, other arithmetic: 1.81 us -> none  [own_panels(): panel.reshape(-1, TILE_ROWS, PANEL) * keep[:, :, None]]
    unnamed x15 -> x7, local copies, waits for them, and re-layouts: 3.36 us -> 3.03 us
  transfers between devices with their start and end apart: 2 -> 0, of which waited for: 2 -> 0; matrix products, arithmetic and copies ran while one was open for 0% -> 0% of each run, Pallas kernels for 0% -> 0%
where the time goes in v2:
time: 45.8 us; the launch traced here: 45.6 us
  Pallas kernels  41.9 us (91%)
  local copies, waits for them, and re-layouts  3.03 us (7%)
  between operations  0.65 us (1%)
    pallas_call x1, Pallas kernels, sums_by_copies(): pl.pallas_call(functools.partial(exchange_kernel, pix_count), out_shape=(...  30.6 us
    pallas_call x1, Pallas kernels, per_device(): pl.pallas_call(update_kernel, out_shape=(jax.ShapeDtypeStruct((rows, cols...  11.3 us
    unnamed x7, local copies, waits for them, and re-layouts  3.03 us

profile of v2, /device:TPU:0, one launch (start us, length us, event | category | flops | bytes accessed | tf_op | source)
XLA Modules:
  0.0 45.6 jit_solution(13090599547728397341)
XLA Ops:
  0.6 0.0 copy-start.2
  0.6 0.8 %copy.8.support_ref = s32[8,4]{1,0:T(8,128)S(1)} copy(s32[8,4]{0,1:T(4,128)} %param.6) | data formatting | bytes 256 | tf_op args[2]
  1.4 0.0 copy-done.2
  1.4 0.0 copy-start
  1.4 1.2 %copy-done = f32[1024,256]{1,0:T(8,128)S(1)} copy-done((f32[1024,256]{1,0:T(8,128)S(1)}, f32[1024,256]{1,0:T(8,128)}, u32[]{:S(2)}) %copy-start) | copy-done | bytes 1048600
  2.6 0.0 copy-start.1
  2.6 1.0 %copy-done.1 = f32[1024,128]{1,0:T(8,128)S(1)} copy-done((f32[1024,128]{1,0:T(8,128)S(1)}, f32[1024,128]{1,0:T(8,128)}, u32[]{:S(2)}) %copy-start.1) | copy-done | bytes 524312
  3.7 30.6 %exchange.1 = (f32[1024,128]{1,0:T(8,128)S(1)}, f32[128,512]{1,0:T(8,128)S(1)}) custom-call(f32[1024,256]{1,0:T(8,128)S(1)} %copy-done, f32[1024,128]{1,0:T(8,128)S(1)} %copy-done.1, s32[8,4]{1,0:T(8,128)S(1)} %copy.8.support_ref, s32[2]{0:T(128)S(1)} %copy-done.2), custom_call_target="tpu_custom_call" | custom-call | tf_op jit(solution)/shard_map/exchange/pallas_call | solution.py:330
  34.3 11.3 %update.1 = (f32[1024,256]{1,0:T(8,128)}, f32[1024,128]{1,0:T(8,128)}, f32[128,128]{1,0:T(8,128)}) custom-call(f32[1024,256]{1,0:T(8,128)S(1)} %copy-done, f32[1024,128]{1,0:T(8,128)S(1)} %copy-done.1, s32[8,4]{1,0:T(8,128)S(1)} %copy.8.support_ref, f32[1024,128]{1,0:T(8,128)S(1)} %get-tuple-element.8.c_ref, f32[128,512]{1,0:T(8,128)S(1)} %get-tuple-element.9.m_ref), custom_call_target="tpu_custom_call" | custom-call | tf_op jit(solution)/shard_map/update/pallas_call | solution.py:364
Async XLA Ops:
  0.6 0.8 %copy-start.2 = (s32[2]{0:T(128)S(1)}, s32[2]{0:T(128)}, u32[]{:S(2)}) copy-start(s32[2]{0:T(128)} %blocks_ref.1) | copy-start | bytes 28
  1.4 1.2 %copy-start = (f32[1024,256]{1,0:T(8,128)S(1)}, f32[1024,256]{1,0:T(8,128)}, u32[]{:S(2)}) copy-start(f32[1024,256]{1,0:T(8,128)} %x_ref.3) | copy-start | bytes 3145732
  2.6 1.0 %copy-start.1 = (f32[1024,128]{1,0:T(8,128)S(1)}, f32[1024,128]{1,0:T(8,128)}, u32[]{:S(2)}) copy-start(f32[1024,128]{1,0:T(8,128)} %y_ref.3) | copy-start | bytes 1572868

commit v3 on v2

--- a/solution.py
+++ b/solution.py
@@ -33,19 +33,29 @@
     lane = lax.broadcasted_iota(jnp.int32, (1, cols), 1)
     row = jnp.zeros((1, cols), jnp.float32)
     for block in range(cols // PANEL):
-        value = support_ref[tile, block].astype(jnp.float32)
+        value = support_ref[block, tile].astype(jnp.float32)
         row = jnp.where((lane >= block * PANEL) & (lane < (block + 1) * PANEL), value, row)
     return row
 
 
-def inverse_factor(work_ref):
+def start_factor(work_ref, gram):
+    row = lax.broadcasted_iota(jnp.int32, (WIDTH, WIDTH), 0)
+    col = lax.broadcasted_iota(jnp.int32, (WIDTH, WIDTH), 1)
+    work_ref[:, :WIDTH] = gram
+    work_ref[:, WIDTH:] = jnp.where(row == col, 1.0, 0.0).astype(jnp.float32)
+
+
+def factor_steps(work_ref, first, last):
     shape = (SUB, WIDTH)
-    sublane = lax.broadcasted_iota(jnp.int32, shape, 0)
-    for block in range(WIDTH // SUB):
-        low = block * SUB
-        rows_g = work_ref[low : low + SUB, :WIDTH]
-        rows_t = work_ref[low : low + SUB, WIDTH:]
-        columns = [jnp.broadcast_to(rows_g[:, low + j : low + j + 1], shape) for j in range(SUB)]
+
+    def step(block, carry):
+        sublane = lax.broadcasted_iota(jnp.int32, shape, 0)
+        row = lax.broadcasted_iota(jnp.int32, (WIDTH, SUB), 0)
+        low = pl.multiple_of(block * SUB, SUB)
+        rows_g = work_ref[pl.ds(low, SUB), :WIDTH]
+        rows_t = work_ref[pl.ds(low, SUB), WIDTH:]
+        turned = pltpu.roll(rows_g, (WIDTH - low) % WIDTH, 1)
+        columns = [jnp.broadcast_to(turned[:, j : j + 1], shape) for j in range(SUB)]
         entry = {
             (i, j): jnp.broadcast_to(columns[j][i : i + 1, :], shape)
             for j in range(SUB)
@@ -68,55 +78,92 @@
                 t[i] = t[i] - entry[i, j] * t[j]
             upper = jnp.where(sublane == j, g[j], upper)
             basis = jnp.where(sublane == j, t[j], basis)
-        work_ref[low : low + SUB, WIDTH:] = basis
-        if low + SUB < WIDTH:
-            both = jnp.concatenate([upper, basis], axis=1)
-            below = upper.T[low + SUB :, :]
-            work_ref[low + SUB :, :] = work_ref[low + SUB :, :] - product(below, both)
-    return work_ref[:, WIDTH:]
+        work_ref[pl.ds(low, SUB), WIDTH:] = basis
+        both = jnp.concatenate([upper, basis], axis=1)
+        below = jnp.where(row >= low + SUB, upper.T, 0.0)
+        work_ref[...] = work_ref[...] - product(below, both)
+        return carry
+
+    lax.fori_loop(first, last, step, 0)
 
 
 def gram_kernel(x_ref, y_ref, support_ref, c_ref, out_ref):
     rows, cols = x_ref.shape
     total = None
     for tile in range(rows // TILE_ROWS):
-        span = pl.ds(tile * TILE_ROWS, TILE_ROWS)
-        masked = x_ref[span, :] * support_row(support_ref, tile, cols)
-        panel = c_ref[span, :]
-        joined = jnp.concatenate([masked, y_ref[span, :], panel], axis=1)
+        panel = c_ref[tile_span(tile), :]
+        masked = masked_tile(x_ref, support_ref, tile)
+        joined = jnp.concatenate([masked, y_ref[tile_span(tile), :], panel], axis=1)
         part = product_t(panel, joined)
         total = part if total is None else total + part
     out_ref[...] = total
 
 
-def update_kernel(x_ref, y_ref, support_ref, c_ref, m_ref, trail_ref, resid_ref, coef_ref, work_ref):
+def factor_kernel(gram_ref, inverse_ref, work_ref):
+    start_factor(work_ref, gram_ref[...])
+    factor_steps(work_ref, 0, WIDTH // SUB)
+    inverse_ref[...] = work_ref[:, WIDTH:]
+
+
+def update_kernel(
+    x_hbm,
+    y_hbm,
+    support_ref,
+    c_ref,
+    m_ref,
+    inverse_ref,
+    trail_hbm,
+    resid_hbm,
+    coef_ref,
+    x_ref,
+    y_ref,
+    trail,
+    resid,
+    in_sem,
+    trail_sem,
+    resid_sem,
+):
     rows, cols = x_ref.shape
-    bands = y_ref.shape[1]
-    row = lax.broadcasted_iota(jnp.int32, (WIDTH, WIDTH), 0)
-    col = lax.broadcasted_iota(jnp.int32, (WIDTH, WIDTH), 1)
-    work_ref[:, :WIDTH] = m_ref[:, cols + bands :]
-    work_ref[:, WIDTH:] = jnp.where(row == col, 1.0, 0.0).astype(jnp.float32)
-    inverse = inverse_factor(work_ref)
-    proj = product(inverse, m_ref[:, : cols + bands])
+    loads = [
+        pltpu.make_async_copy(x_hbm, x_ref, in_sem.at[0]),
+        pltpu.make_async_copy(y_hbm, y_ref, in_sem.at[1]),
+    ]
+    for copy in loads:
+        copy.start()
+    inverse = inverse_ref[...]
+    proj = product(inverse, m_ref[...])
     coef_ref[...] = proj[:, cols:]
     weights = product_t(inverse, proj)
+    for copy in loads:
+        copy.wait()
+    stores = []
     for tile in range(rows // TILE_ROWS):
         span = pl.ds(tile * TILE_ROWS, TILE_ROWS)
-        masked = x_ref[span, :] * support_row(support_ref, tile, cols)
         change = product(c_ref[span, :], weights)
-        trail_ref[span, :] = masked - change[:, :cols]
-        resid_ref[span, :] = y_ref[span, :] - change[:, cols:]
+        trail[span, :] = masked_tile(x_ref, support_ref, tile) - change[:, :cols]
+        resid[span, :] = y_ref[span, :] - change[:, cols:]
+        stores.append(pltpu.make_async_copy(trail.at[span, :], trail_hbm.at[span, :], trail_sem.at[tile]))
+        stores.append(pltpu.make_async_copy(resid.at[span, :], resid_hbm.at[span, :], resid_sem.at[tile]))
+        stores[-2].start()
+        stores[-1].start()
+    for copy in stores:
+        copy.wait()
+
+
+def tile_span(tile):
+    start = tile * TILE_ROWS
+    return pl.ds(start if isinstance(start, int) else pl.multiple_of(start, TILE_ROWS), TILE_ROWS)
 
 
 def masked_tile(x_ref, support_ref, tile):
-    span = pl.ds(pl.multiple_of(tile * TILE_ROWS, TILE_ROWS), TILE_ROWS)
+    span = tile_span(tile)
     return x_ref[span, :] * support_row(support_ref, tile, x_ref.shape[1])
 
 
 def own_panel_tile(x_ref, support_ref, blocks_ref, holder, tile):
     cols = x_ref.shape[1]
     blocks_here = cols // PANEL
-    span = pl.ds(pl.multiple_of(tile * TILE_ROWS, TILE_ROWS), TILE_ROWS)
+    span = tile_span(tile)
     left = lax.broadcasted_iota(jnp.int32, (1, WIDTH), 1) < PANEL
     total = jnp.zeros((TILE_ROWS, WIDTH), jnp.float32)
     for pair in range(cols // WIDTH):
@@ -125,7 +172,7 @@
         factors = []
         for half in range(2):
             local = pair * 2 + half
-            keep = support_ref[tile, local].astype(jnp.float32)
+            keep = support_ref[local, tile].astype(jnp.float32)
             factors.append(
                 [jnp.where(blocks_ref[i] == holder * blocks_here + local, keep, 0.0) for i in range(2)]
             )
@@ -137,18 +184,26 @@
 
 def exchange_kernel(
     pix_count,
-    x_ref,
-    y_ref,
+    x_hbm,
+    y_hbm,
     support_ref,
     blocks_ref,
     c_ref,
     m_ref,
+    inverse_ref,
+    x_ref,
+    y_ref,
     own,
     first_in,
     chip_sum,
     second_in,
+    gram_part,
+    gram,
+    gram_slots,
     acc,
     slots,
+    work_ref,
+    in_sem,
     send1,
     recv1,
     send2,
@@ -159,6 +214,10 @@
     recv4,
     send5,
     recv5,
+    send6,
+    recv6,
+    send7,
+    recv7,
 ):
     rows, cols = x_ref.shape
     half = rows // 2
@@ -169,6 +228,20 @@
     beside = eb + 1 - 2 * core
     across = (eb + 2) % 4
     others = [(pix + d) % pix_count for d in range(1, pix_count)]
+
+    def side_of(ref, side):
+        return ref.at[pl.ds(pl.multiple_of(side * half, TILE_ROWS), half), :]
+
+    loads = []
+    for index, (src, dst) in enumerate(
+        [
+            (side_of(x_hbm, 1 - core), side_of(x_ref, 1 - core)),
+            (side_of(x_hbm, core), side_of(x_ref, core)),
+            (y_hbm, y_ref),
+        ]
+    ):
+        loads.append(pltpu.make_async_copy(src, dst, in_sem.at[index]))
+        loads[-1].start()
 
     barrier = pltpu.get_barrier_semaphore()
     for target in [(pix, beside), (pix, across)] + [(other, eb) for other in others]:
@@ -197,17 +270,19 @@
         tile = side * chunks + chunk
         own[span(side, chunk), :] = own_panel_tile(x_ref, support_ref, blocks_ref, eb, tile)
 
+    def accumulate_gram(side, chunk, first):
+        panel = c_ref[span(side, chunk), :]
+        part = product_t(panel, panel)
+        gram_part[...] = part if first else gram_part[...] + part
+
     def accumulate(side, chunk, first):
         panel = c_ref[span(side, chunk), :]
         masked = masked_tile(x_ref, support_ref, side * chunks + chunk)
-        joined = jnp.concatenate([masked, y_ref[span(side, chunk), :], panel], axis=1)
-        part = product_t(panel, joined)
-        if first:
-            acc[...] = part
-        else:
-            acc[...] += part
+        part = product_t(panel, jnp.concatenate([masked, y_ref[span(side, chunk), :]], axis=1))
+        acc[...] = part if first else acc[...] + part
 
     other_core = 1 - core
+    loads[0].wait()
     prepare(other_core, 0)
     pl.semaphore_wait(barrier, pix_count + 1)
     copies1 = []
@@ -223,8 +298,10 @@
                 (pix, beside),
             )
         )
+    loads[1].wait()
     for chunk in range(chunks):
         prepare(core, chunk)
+    loads[2].wait()
 
     copies2 = []
     for chunk in range(chunks):
@@ -253,41 +330,68 @@
                 (pix, beside),
             )
         )
-        accumulate(core, chunk, chunk == 0)
+        accumulate_gram(core, chunk, chunk == 0)
+        if chunk < chunks - 1:
+            accumulate(core, chunk, chunk == 0)
         if chunk > 0:
             copies3[chunk - 1].wait_recv()
-            accumulate(other_core, chunk - 1, False)
+            accumulate_gram(other_core, chunk - 1, False)
+            if chunk < chunks - 1:
+                accumulate(other_core, chunk - 1, False)
     copies3[chunks - 1].wait_recv()
+    accumulate_gram(other_core, chunks - 1, False)
+
+    share = WIDTH // pix_count
+    mine = pl.ds(pl.multiple_of(pix * share, share), share)
+
+    def scatter(part, landing, send_sem, recv_sem):
+        copies = []
+        for index, other in enumerate(others):
+            rows_there = pl.ds(pl.multiple_of(other * share, share), share)
+            copies.append(
+                send(part.at[rows_there, :], landing.at[index], send_sem.at[index], recv_sem.at[index], (other, eb))
+            )
+        return copies
+
+    def add_up(part, landing, copies):
+        total = part[mine, :]
+        for index in range(pix_count - 1):
+            copies[index].wait_recv()
+            total = total + landing[index]
+        return total
+
+    def gather(ref, send_sem, recv_sem):
+        return [
+            send(ref.at[mine, :], ref.at[mine, :], send_sem.at[index], recv_sem.at[index], (other, eb))
+            for index, other in enumerate(others)
+        ]
+
+    copies4 = scatter(gram_part, gram_slots, send4, recv4)
+    accumulate(core, chunks - 1, chunks == 1)
+    if chunks > 1:
+        accumulate(other_core, chunks - 2, False)
     accumulate(other_core, chunks - 1, False)
-
-    share = WIDTH // pix_count
-
-    def rows_of(index):
-        return pl.ds(pl.multiple_of(index * share, share), share)
-
-    copies4 = []
-    for index, other in enumerate(others):
-        copies4.append(
-            send(acc.at[rows_of(other), :], slots.at[index], send4.at[index], recv4.at[index], (other, eb))
-        )
-    total = acc[rows_of(pix), :]
-    for index in range(pix_count - 1):
-        copies4[index].wait_recv()
-        total = total + slots[index]
-    m_ref[rows_of(pix), :] = total
-    copies5 = []
-    for index, other in enumerate(others):
-        copies5.append(
-            send(m_ref.at[rows_of(pix), :], m_ref.at[rows_of(pix), :], send5.at[index], recv5.at[index], (other, eb))
-        )
+    gram[mine, :] = add_up(gram_part, gram_slots, copies4)
+    copies5 = gather(gram, send5, recv5)
+    copies6 = scatter(acc, slots, send6, recv6)
     for copy in copies5:
         copy.wait_recv()
-    for copy in copies1 + copies2 + copies3 + copies4 + copies5:
+    start_factor(work_ref, gram[...])
+    steps = WIDTH // SUB
+    factor_steps(work_ref, 0, steps // 2)
+    m_ref[mine, :] = add_up(acc, slots, copies6)
+    copies7 = gather(m_ref, send7, recv7)
+    factor_steps(work_ref, steps // 2, steps)
+    inverse_ref[...] = work_ref[:, WIDTH:]
+    for copy in copies7:
+        copy.wait_recv()
+    for copy in copies1 + copies2 + copies3 + copies4 + copies5 + copies6 + copies7:
         copy.wait_send()
 
 
 VMEM = pl.BlockSpec(memory_space=pltpu.VMEM)
 SMEM = pl.BlockSpec(memory_space=pltpu.SMEM)
+HBM = pl.BlockSpec(memory_space=pltpu.HBM)
 
 
 def own_panels(abundance, support, panel_blocks, holder):
@@ -306,7 +410,7 @@
 def sums_by_collectives(abundance, spectra, support, panel_blocks):
     cols = abundance.shape[1]
     bands = spectra.shape[1]
-    own = own_panels(abundance, support, panel_blocks, lax.axis_index("eb"))
+    own = own_panels(abundance, support.T, panel_blocks, lax.axis_index("eb"))
     panels = lax.psum(own, "eb")
     grams = pl.pallas_call(
         gram_kernel,
@@ -316,32 +420,50 @@
         compiler_params=pltpu.CompilerParams(vmem_limit_bytes=VMEM_LIMIT),
         name="gram",
     )(abundance, spectra, support, panels)
-    return panels, lax.psum(grams, "pix")
+    grams = lax.psum(grams, "pix")
+    inverse = pl.pallas_call(
+        factor_kernel,
+        out_shape=jax.ShapeDtypeStruct((WIDTH, WIDTH), jnp.float32),
+        in_specs=[VMEM],
+        out_specs=VMEM,
+        scratch_shapes=[pltpu.VMEM((WIDTH, 2 * WIDTH), jnp.float32)],
+        compiler_params=pltpu.CompilerParams(vmem_limit_bytes=VMEM_LIMIT),
+        name="factor",
+    )(grams[:, cols + bands :])
+    return panels, grams[:, : cols + bands], inverse
 
 
 def sums_by_copies(pix_count, abundance, spectra, support, panel_blocks):
     rows, cols = abundance.shape
-    width = cols + spectra.shape[1] + WIDTH
+    width = cols + spectra.shape[1]
     half = rows // 2
     chunks = half // TILE_ROWS
     dma = pltpu.SemaphoreType.DMA
     near = [dma((chunks,))] * 6
-    far = [dma((pix_count - 1,))] * 4
+    far = [dma((pix_count - 1,))] * 8
     return pl.pallas_call(
         functools.partial(exchange_kernel, pix_count),
         out_shape=(
             jax.ShapeDtypeStruct((rows, WIDTH), jnp.float32),
             jax.ShapeDtypeStruct((WIDTH, width), jnp.float32),
+            jax.ShapeDtypeStruct((WIDTH, WIDTH), jnp.float32),
         ),
-        in_specs=[VMEM, VMEM, SMEM, SMEM],
-        out_specs=(VMEM, VMEM),
+        in_specs=[HBM, HBM, SMEM, SMEM],
+        out_specs=(VMEM, VMEM, VMEM),
         scratch_shapes=[
+            pltpu.VMEM(abundance.shape, jnp.float32),
+            pltpu.VMEM(spectra.shape, jnp.float32),
             pltpu.VMEM((rows, WIDTH), jnp.float32),
             pltpu.VMEM((half, WIDTH), jnp.float32),
             pltpu.VMEM((half, WIDTH), jnp.float32),
             pltpu.VMEM((half, WIDTH), jnp.float32),
+            pltpu.VMEM((WIDTH, WIDTH), jnp.float32),
+            pltpu.VMEM((WIDTH, WIDTH), jnp.float32),
+            pltpu.VMEM((pix_count - 1, WIDTH // pix_count, WIDTH), jnp.float32),
             pltpu.VMEM((WIDTH, width), jnp.float32),
             pltpu.VMEM((pix_count - 1, WIDTH // pix_count, width), jnp.float32),
+            pltpu.VMEM((WIDTH, 2 * WIDTH), jnp.float32),
+            dma((3,)),
         ]
         + near
         + far,
@@ -355,11 +477,12 @@
 def per_device(pix_count, eb_count, abundance, spectra, support, panel_blocks):
     rows, cols = abundance.shape
     bands = spectra.shape[1]
+    support = support.T
     args = (abundance, spectra, support, panel_blocks)
     if eb_count == 4 and 1 < pix_count and WIDTH % (SUB * pix_count) == 0:
-        panels, grams = sums_by_copies(pix_count, *args)
+        panels, grams, inverse = sums_by_copies(pix_count, *args)
     else:
-        panels, grams = sums_by_collectives(*args)
+        panels, grams, inverse = sums_by_collectives(*args)
     params = pltpu.CompilerParams(vmem_limit_bytes=VMEM_LIMIT)
     trailing, residual, coefficients = pl.pallas_call(
         update_kernel,
@@ -368,12 +491,20 @@
             jax.ShapeDtypeStruct((rows, bands), jnp.float32),
             jax.ShapeDtypeStruct((WIDTH, bands), jnp.float32),
         ),
-        in_specs=[VMEM, VMEM, SMEM, VMEM, VMEM],
-        out_specs=(VMEM, VMEM, VMEM),
-        scratch_shapes=[pltpu.VMEM((WIDTH, 2 * WIDTH), jnp.float32)],
+        in_specs=[HBM, HBM, SMEM, VMEM, VMEM, VMEM],
+        out_specs=(HBM, HBM, VMEM),
+        scratch_shapes=[
+            pltpu.VMEM((rows, cols), jnp.float32),
+            pltpu.VMEM((rows, bands), jnp.float32),
+            pltpu.VMEM((rows, cols), jnp.float32),
+            pltpu.VMEM((rows, bands), jnp.float32),
+            pltpu.SemaphoreType.DMA((2,)),
+            pltpu.SemaphoreType.DMA((rows // TILE_ROWS,)),
+            pltpu.SemaphoreType.DMA((rows // TILE_ROWS,)),
+        ],
         compiler_params=params,
         name="update",
-    )(abundance, spectra, support, panels, grams)
+    )(abundance, spectra, support, panels, grams, inverse)
     return trailing, residual, coefficients.reshape(NPANELS, PANEL, bands)
 
 

time: 45.8 us -> 44.8 us (0.978)
  Pallas kernels: 41.9 us -> 40.3 us
  local copies, waits for them, and re-layouts: 3.03 us -> 3.59 us
    pallas_call x1, Pallas kernels: 11.3 us -> 4.21 us  [per_device(): pl.pallas_call(update_kernel, out_shape=(jax.ShapeDtypeStruct((rows, cols...]
    pallas_call x1, Pallas kernels: 30.6 us -> 36.1 us  [sums_by_copies(): pl.pallas_call(functools.partial(exchange_kernel, pix_count), out_shape=(...]
    unnamed x7 -> x8, local copies, waits for them, and re-layouts: 3.03 us -> 3.59 us
where the time goes in v3:
time: 44.8 us; the launch traced here: 44.5 us
  Pallas kernels  40.3 us (90%)
  local copies, waits for them, and re-layouts  3.59 us (8%)
  between operations  0.65 us (1%)
    pallas_call x1, Pallas kernels, sums_by_copies(): pl.pallas_call(functools.partial(exchange_kernel, pix_count), out_shape=(...  36.1 us
    pallas_call x1, Pallas kernels, per_device(): pl.pallas_call(update_kernel, out_shape=(jax.ShapeDtypeStruct((rows, cols...  4.21 us
    unnamed x8, local copies, waits for them, and re-layouts  3.59 us

profile of v3, /device:TPU:0, one launch (start us, length us, event | category | flops | bytes accessed | tf_op | source)
XLA Modules:
  0.0 44.5 jit_solution(5896701846993200563)
XLA Ops:
  0.6 0.0 copy-start.3
  0.6 0.6 %copy-done.3 = s32[2]{0:T(128)S(1)} copy-done((s32[2]{0:T(128)S(1)}, s32[2]{0:T(128)}, u32[]{:S(2)}) %copy-start.3) | copy-done | bytes 32
  1.3 0.0 copy-start
  1.3 1.2 %copy-done = f32[1024,256]{1,0:T(8,128)S(1)} copy-done((f32[1024,256]{1,0:T(8,128)S(1)}, f32[1024,256]{1,0:T(8,128)}, u32[]{:S(2)}) %copy-start) | copy-done | bytes 1048600
  2.5 0.0 copy-start.1
  2.5 1.0 %copy-done.1 = f32[1024,128]{1,0:T(8,128)S(1)} copy-done((f32[1024,128]{1,0:T(8,128)S(1)}, f32[1024,128]{1,0:T(8,128)}, u32[]{:S(2)}) %copy-start.1) | copy-done | bytes 524312
  3.6 0.0 copy-start.2
  3.6 0.7 %copy-done.2 = s32[8,4]{0,1:T(4,128)S(1)} copy-done((s32[8,4]{0,1:T(4,128)S(1)}, s32[8,4]{0,1:T(4,128)}, u32[]{:S(2)}) %copy-start.2) | copy-done | bytes 152
  4.2 36.1 %exchange.1 = (f32[1024,128]{1,0:T(8,128)S(1)}, f32[128,384]{1,0:T(8,128)S(1)}, f32[128,128]{1,0:T(8,128)S(1)}) custom-call(f32[1024,256]{1,0:T(8,128)S(1)} %copy-done, f32[1024,128]{1,0:T(8,128)S(1)} %copy-done.1, s32[4,8]{1,0:T(4,128)S(1)} %bitcast.2, s32[2]{0:T(128)S(1)} %copy-done.3), custom_call_target="tpu_custom_call" | custom-call | tf_op jit(solution)/shard_map/exchange/pallas_call | solution.py:444
  40.3 4.2 %update.1 = (f32[1024,256]{1,0:T(8,128)}, f32[1024,128]{1,0:T(8,128)}, f32[128,128]{1,0:T(8,128)}) custom-call(f32[1024,256]{1,0:T(8,128)S(1)} %copy-done, f32[1024,128]{1,0:T(8,128)S(1)} %copy-done.1, s32[4,8]{1,0:T(4,128)S(1)} %bitcast.3, f32[1024,128]{1,0:T(8,128)S(1)} %get-tuple-element.9.c_ref, f32[128,384]{1,0:T(8,128)S(1)} %get-tuple-element.10.m_ref, ...), custom_call_target="tpu_custom_call" | custom-call | tf_op jit(solution)/shard_map/update/pallas_call | solution.py:487
Async XLA Ops:
  0.6 0.7 %copy-start.3 = (s32[2]{0:T(128)S(1)}, s32[2]{0:T(128)}, u32[]{:S(2)}) copy-start(s32[2]{0:T(128)} %blocks_ref.1) | copy-start | bytes 28
  1.3 1.2 %copy-start = (f32[1024,256]{1,0:T(8,128)S(1)}, f32[1024,256]{1,0:T(8,128)}, u32[]{:S(2)}) copy-start(f32[1024,256]{1,0:T(8,128)} %x_hbm.3) | copy-start | bytes 3145732
  2.5 1.0 %copy-start.1 = (f32[1024,128]{1,0:T(8,128)S(1)}, f32[1024,128]{1,0:T(8,128)}, u32[]{:S(2)}) copy-start(f32[1024,128]{1,0:T(8,128)} %y_hbm.3) | copy-start | bytes 1572868
  3.6 0.7 %copy-start.2 = (s32[8,4]{0,1:T(4,128)S(1)}, s32[8,4]{0,1:T(4,128)}, u32[]{:S(2)}) copy-start(s32[8,4]{0,1:T(4,128)} %param.6) | copy-start | bytes 388

commit v4 on v3

v4 whole, which is shorter than its diff:
```python
import functools

import jax
import jax.numpy as jnp
from jax import lax
from jax.experimental import pallas as pl
from jax.experimental.pallas import tpu as pltpu
from jax.sharding import PartitionSpec as P

PANEL = 64
TILE_ROWS = 128
NPANELS = 2
WIDTH = PANEL * NPANELS
SUB = 8
VMEM_LIMIT = 48 * 1024 * 1024
EXCHANGE_VMEM = 64 * 1024 * 1024 - 512 * 1024


def product(left, right):
    return jnp.dot(left, right, precision=lax.Precision.HIGHEST, preferred_element_type=jnp.float32)


def product_t(left, right):
    return lax.dot_general(
        left,
        right,
        (((0,), (0,)), ((), ())),
        precision=lax.Precision.HIGHEST,
        preferred_element_type=jnp.float32,
    )


def product_nt(left, right):
    return lax.dot_general(
        left,
        right,
        (((1,), (1,)), ((), ())),
        precision=lax.Precision.HIGHEST,
        preferred_element_type=jnp.float32,
    )


def support_row(support_ref, tile, cols):
    lane = lax.broadcasted_iota(jnp.int32, (1, cols), 1)
    row = jnp.zeros((1, cols), jnp.float32)
    for block in range(cols // PANEL):
        value = support_ref[block, tile].astype(jnp.float32)
        row = jnp.where((lane >= block * PANEL) & (lane < (block + 1) * PANEL), value, row)
    return row


def factor_steps(work_ref, first, last):
    shape = (SUB, WIDTH)

    def step(block, carry):
        sublane = lax.broadcasted_iota(jnp.int32, shape, 0)
        row = lax.broadcasted_iota(jnp.int32, (PANEL, SUB), 0)
        low = pl.multiple_of(block * SUB, SUB)
        rows = work_ref[pl.ds(low, SUB), :]
        turned = pltpu.roll(rows, (WIDTH - low) % WIDTH, 1)
        columns = [jnp.broadcast_to(turned[:, j : j + 1], shape) for j in range(SUB)]
        entry = {
            (i, j): jnp.broadcast_to(columns[j][i : i + 1, :], shape)
            for j in range(SUB)
            for i in range(j, SUB)
        }
        g = [jnp.broadcast_to(rows[i : i + 1, :], shape) for i in range(SUB)]
        upper = rows
        for j in range(SUB):
            scale = lax.rsqrt(entry[j, j])
            for i in range(j + 1, SUB):
                entry[i, j] = entry[i, j] * scale
            g[j] = g[j] * scale
            for i in range(j + 1, SUB):
                for k in range(j + 1, i + 1):
                    entry[i, k] = entry[i, k] - entry[i, j] * entry[k, j]
                g[i] = g[i] - entry[i, j] * g[j]
            upper = jnp.where(sublane == j, g[j], upper)
        below = jnp.where(row >= low + SUB, upper.T[:PANEL, :], 0.0)
        work_ref[...] = work_ref[...] - product(below, upper)
        work_ref[pl.ds(low, SUB), :] = upper
        return carry

    lax.fori_loop(first, last, step, 0)


def inverse_factor(work_ref, gram):
    row = lax.broadcasted_iota(jnp.int32, (PANEL, PANEL), 0)
    col = lax.broadcasted_iota(jnp.int32, (PANEL, PANEL), 1)
    work_ref[...] = jnp.concatenate([gram, jnp.where(row == col, 1.0, 0.0)], axis=1)
    factor_steps(work_ref, 0, PANEL // SUB)
    return work_ref[:, PANEL:]


def second_factor(work_ref, inverse0, grams1, inverse_ref):
    coupling = product_nt(grams1[:, :PANEL], inverse0)
    remainder = grams1[:, PANEL:] - product_nt(coupling, coupling)
    carried = product(coupling, inverse0)
    inverse_ref[:PANEL, :] = jnp.concatenate([inverse0, jnp.zeros_like(inverse0)], axis=1)
    inverse1 = inverse_factor(work_ref, remainder)
    inverse_ref[PANEL:, :] = jnp.concatenate([-product(inverse1, carried), inverse1], axis=1)


def gram_kernel(x_ref, y_ref, support_ref, c_ref, out_ref):
    rows, cols = x_ref.shape
    total = None
    for tile in range(rows // TILE_ROWS):
        panel = c_ref[tile_span(tile), :]
        masked = masked_tile(x_ref, support_ref, tile)
        joined = jnp.concatenate([masked, y_ref[tile_span(tile), :], panel], axis=1)
        part = product_t(panel, joined)
        total = part if total is None else total + part
    out_ref[...] = total


def factor_kernel(gram_ref, inverse_ref, work_ref):
    inverse0 = inverse_factor(work_ref, gram_ref[:PANEL, :PANEL])
    second_factor(work_ref, inverse0, gram_ref[PANEL:, :], inverse_ref)


def update_kernel(
    x_hbm,
    y_hbm,
    support_ref,
    c_hbm,
    m_ref,
    inverse_ref,
    trail_hbm,
    resid_hbm,
    coef_ref,
    x_ref,
    y_ref,
    c_ref,
    trail,
    resid,
    in_sem,
    trail_sem,
    resid_sem,
):
    rows, cols = x_ref.shape
    loads = [
        pltpu.make_async_copy(x_hbm, x_ref, in_sem.at[0]),
        pltpu.make_async_copy(y_hbm, y_ref, in_sem.at[1]),
        pltpu.make_async_copy(c_hbm, c_ref, in_sem.at[2]),
    ]
    for copy in loads:
        copy.start()
    inverse = inverse_ref[...]
    share = m_ref.shape[1] // NPANELS
    sums = jnp.concatenate(
        [m_ref[p, i * share : (i + 1) * share, :] for i in range(NPANELS) for p in range(m_ref.shape[0])], axis=0
    )
    proj = product(inverse, sums)
    coef_ref[...] = proj[:, cols:]
    weights = product_t(inverse, proj)
    for copy in loads:
        copy.wait()
    stores = []
    for tile in range(rows // TILE_ROWS):
        span = pl.ds(tile * TILE_ROWS, TILE_ROWS)
        change = product(c_ref[span, :], weights)
        trail[span, :] = masked_tile(x_ref, support_ref, tile) - change[:, :cols]
        resid[span, :] = y_ref[span, :] - change[:, cols:]
        stores.append(pltpu.make_async_copy(trail.at[span, :], trail_hbm.at[span, :], trail_sem.at[tile]))
        stores.append(pltpu.make_async_copy(resid.at[span, :], resid_hbm.at[span, :], resid_sem.at[tile]))
        stores[-2].start()
        stores[-1].start()
    for copy in stores:
        copy.wait()


def tile_span(tile):
    start = tile * TILE_ROWS
    return pl.ds(start if isinstance(start, int) else pl.multiple_of(start, TILE_ROWS), TILE_ROWS)


def masked_tile(x_ref, support_ref, tile):
    span = tile_span(tile)
    return x_ref[span, :] * support_row(support_ref, tile, x_ref.shape[1])


def own_panel_pair(x_ref, support_ref, blocks_ref, holder, tile):
    blocks_here = x_ref.shape[1] // PANEL
    left = lax.broadcasted_iota(jnp.int32, (1, WIDTH), 1) < PANEL
    totals = [jnp.zeros((TILE_ROWS, WIDTH), jnp.float32) for _ in range(NPANELS)]
    for place in range(2):
        for pair in range(blocks_here // 2):
            values = x_ref[tile_span(tile + place), pair * WIDTH : (pair + 1) * WIDTH]
            turned = pltpu.roll(values, PANEL, 1)
            for half in range(2):
                local = pair * 2 + half
                keep = support_ref[local, tile + place].astype(jnp.float32)
                source = values if half == place else turned
                for index in range(NPANELS):
                    factor = jnp.where(blocks_ref[index] == holder * blocks_here + local, keep, 0.0)
                    lanes = jnp.where(left, factor, 0.0) if place == 0 else jnp.where(left, 0.0, factor)
                    totals[index] = totals[index] + source * lanes
    return totals


def exchange_kernel(
    pix_count,
    x_hbm,
    y_hbm,
    support_ref,
    blocks_ref,
    c_hbm,
    m_ref,
    inverse_ref,
    x_ref,
    y_ref,
    c_ref,
    own,
    first_in,
    chip_sum,
    second_in,
    full,
    gram0_part,
    gram0,
    gram0_slots,
    gram1_part,
    gram1,
    gram1_slots,
    m0_part,
    m0_slots,
    m1_part,
    m1_slots,
    work_ref,
    in_sem,
    out_sem,
    send1,
    recv1,
    send2,
    recv2,
    send3,
    recv3,
    gram0_sems,
    gram1_sems,
    m0_sems,
    m1_sems,
    gather_sems,
):
    rows, cols = x_ref.shape
    half = rows // 2
    chunks = half // (2 * TILE_ROWS)
    pix = lax.axis_index("pix")
    eb = lax.axis_index("eb")
    core = eb % 2
    other_core = 1 - core
    beside = eb + 1 - 2 * core
    across = (eb + 2) % 4
    others = [(pix + d) % pix_count for d in range(1, pix_count)]

    def side_of(ref, side):
        return ref.at[pl.ds(pl.multiple_of(side * half, TILE_ROWS), half), :]

    loads = []
    for index, (src, dst) in enumerate(
        [
            (side_of(x_hbm, other_core), side_of(x_ref, other_core)),
            (side_of(x_hbm, core), side_of(x_ref, core)),
            (y_hbm, y_ref),
        ]
    ):
        loads.append(pltpu.make_async_copy(src, dst, in_sem.at[index]))
        loads[-1].start()

    barrier = pltpu.get_barrier_semaphore()
    for target in [(pix, beside), (pix, across)] + [(other, eb) for other in others]:
        pl.semaphore_signal(barrier, inc=1, device_id=target, device_id_type=pl.DeviceIdType.MESH)

    started = []

    def send(src, dst, send_sem, recv_sem, target):
        copy = pltpu.make_async_remote_copy(
            src_ref=src,
            dst_ref=dst,
            send_sem=send_sem,
            recv_sem=recv_sem,
            device_id=target,
            device_id_type=pl.DeviceIdType.MESH,
        )
        copy.start()
        started.append(copy)
        return copy

    def prepare(side, chunk):
        pair = side * chunks + chunk
        for index, values in enumerate(own_panel_pair(x_ref, support_ref, blocks_ref, eb, pair * 2)):
            own[index, pair] = values

    def pair_span(pair):
        return pl.ds(pl.multiple_of(pair * (2 * TILE_ROWS), 2 * TILE_ROWS), 2 * TILE_ROWS)

    def unpack(index, pair):
        packed = full[index, pair]
        lanes = slice(index * PANEL, (index + 1) * PANEL)
        c_ref[tile_span(pair * 2), lanes] = packed[:, :PANEL]
        c_ref[tile_span(pair * 2 + 1), lanes] = packed[:, PANEL:]

    def add_gram(index, pair, part, first):
        panel = c_ref[pair_span(pair), index * PANEL : (index + 1) * PANEL]
        value = product_t(panel, c_ref[pair_span(pair), :])
        part[...] = value if first else part[...] + value

    def add_products(index, part):
        total = None
        for pair in range(2 * chunks):
            panel = c_ref[pair * 2 * TILE_ROWS : (pair + 1) * 2 * TILE_ROWS, index * PANEL : (index + 1) * PANEL]
            masked = jnp.concatenate(
                [masked_tile(x_ref, support_ref, pair * 2 + place) for place in range(2)], axis=0
            )
            values = y_ref[pair * 2 * TILE_ROWS : (pair + 1) * 2 * TILE_ROWS, :]
            value = product_t(panel, jnp.concatenate([masked, values], axis=1))
            total = value if total is None else total + value
        part[...] = total

    share = PANEL // pix_count
    mine = pl.ds(pl.multiple_of(pix * share, share), share)

    def scatter(part, landing, sems):
        copies = []
        for index, other in enumerate(others):
            rows_there = pl.ds(pl.multiple_of(other * share, share), share)
            copies.append(
                send(part.at[rows_there, :], landing.at[index], sems.at[0, index], sems.at[1, index], (other, eb))
            )
        return copies

    def add_up(part, landing, copies):
        total = part[mine, :]
        for index in range(pix_count - 1):
            copies[index].wait_recv()
            total = total + landing[index]
        return total

    def gather(block, sems, place):
        return [
            send(block, block, sems.at[place, index], sems.at[place + 1, index], (other, eb))
            for index, other in enumerate(others)
        ]

    def arrive(index):
        part = gram0_part if index == 0 else gram1_part
        copies3 = []
        for chunk in range(chunks):
            copies2[index][chunk].wait_recv()
            pair = core * chunks + chunk
            full[index, pair] = chip_sum[index, chunk] + second_in[index, chunk]
            copies3.append(
                send(
                    full.at[index, pair],
                    full.at[index, pair],
                    send3.at[index, chunk],
                    recv3.at[index, chunk],
                    (pix, beside),
                )
            )
            unpack(index, pair)
            add_gram(index, pair, part, chunk == 0)
        for chunk in range(chunks):
            copies3[chunk].wait_recv()
            pair = other_core * chunks + chunk
            unpack(index, pair)
            add_gram(index, pair, part, False)

    c_ref[...] = jnp.zeros_like(c_ref)
    loads[0].wait()
    for chunk in range(chunks):
        prepare(other_core, chunk)
    pl.semaphore_wait(barrier, pix_count + 1)
    copies1 = [
        [
            send(
                own.at[index, other_core * chunks + chunk],
                first_in.at[index, chunk],
                send1.at[index, chunk],
                recv1.at[index, chunk],
                (pix, beside),
            )
            for chunk in range(chunks)
        ]
        for index in range(NPANELS)
    ]
    loads[1].wait()
    for chunk in range(chunks):
        prepare(core, chunk)
    copies2 = []
    for index in range(NPANELS):
        copies2.append([])
        for chunk in range(chunks):
            copies1[index][chunk].wait_recv()
            chip_sum[index, chunk] = own[index, core * chunks + chunk] + first_in[index, chunk]
            copies2[index].append(
                send(
                    chip_sum.at[index, chunk],
                    second_in.at[index, chunk],
                    send2.at[index, chunk],
                    recv2.at[index, chunk],
                    (pix, across),
                )
            )
    loads[2].wait()

    arrive(0)
    gram0_copies = scatter(gram0_part, gram0_slots, gram0_sems)
    add_products(0, m0_part)
    gram0[mine, :] = add_up(gram0_part, gram0_slots, gram0_copies)
    gram0_gather = gather(gram0.at[mine, :], gram0_sems, 2)
    m0_copies = scatter(m0_part, m0_slots, m0_sems)

    arrive(1)
    gram1_copies = scatter(gram1_part, gram1_slots, gram1_sems)
    keep_c = pltpu.make_async_copy(c_ref, c_hbm, out_sem)
    keep_c.start()
    add_products(1, m1_part)
    gram1[mine, :] = add_up(gram1_part, gram1_slots, gram1_copies)
    gram1_gather = gather(gram1.at[mine, :], gram1_sems, 2)
    m1_copies = scatter(m1_part, m1_slots, m1_sems)

    for copy in gram0_gather:
        copy.wait_recv()
    inverse0 = inverse_factor(work_ref, gram0[:, :PANEL])
    m_ref[pix, :share, :] = add_up(m0_part, m0_slots, m0_copies)
    m_ref[pix, share:, :] = add_up(m1_part, m1_slots, m1_copies)
    m_gather = gather(m_ref.at[pix], gather_sems, 0)
    for copy in gram1_gather:
        copy.wait_recv()
    second_factor(work_ref, inverse0, gram1[...], inverse_ref)
    for copy in m_gather:
        copy.wait_recv()
    for copy in started:
        copy.wait_send()
    keep_c.wait()


VMEM = pl.BlockSpec(memory_space=pltpu.VMEM)
SMEM = pl.BlockSpec(memory_space=pltpu.SMEM)
HBM = pl.BlockSpec(memory_space=pltpu.HBM)


def own_panels(abundance, support, panel_blocks, holder):
    blocks_here = abundance.shape[1] // PANEL
    parts = []
    for index in range(NPANELS):
        block = panel_blocks[index]
        local = block % blocks_here
        panel = lax.dynamic_slice_in_dim(abundance, local * PANEL, PANEL, 1)
        keep = lax.dynamic_slice_in_dim(support, local, 1, 1).astype(jnp.float32)
        keep = jnp.where(block // blocks_here == holder, keep, 0.0)
        parts.append((panel.reshape(-1, TILE_ROWS, PANEL) * keep[:, :, None]).reshape(-1, PANEL))
    return jnp.concatenate(parts, axis=1)


def sums_by_collectives(abundance, spectra, support, panel_blocks):
    cols = abundance.shape[1]
    bands = spectra.shape[1]
    own = own_panels(abundance, support.T, panel_blocks, lax.axis_index("eb"))
    panels = lax.psum(own, "eb")
    grams = pl.pallas_call(
        gram_kernel,
        out_shape=jax.ShapeDtypeStruct((WIDTH, cols + bands + WIDTH), jnp.float32),
        in_specs=[VMEM, VMEM, SMEM, VMEM],
        out_specs=VMEM,
        compiler_params=pltpu.CompilerParams(vmem_limit_bytes=VMEM_LIMIT),
        name="gram",
    )(abundance, spectra, support, panels)
    grams = lax.psum(grams, "pix")
    inverse = pl.pallas_call(
        factor_kernel,
        out_shape=jax.ShapeDtypeStruct((WIDTH, WIDTH), jnp.float32),
        in_specs=[VMEM],
        out_specs=VMEM,
        scratch_shapes=[pltpu.VMEM((PANEL, WIDTH), jnp.float32)],
        compiler_params=pltpu.CompilerParams(vmem_limit_bytes=VMEM_LIMIT),
        name="factor",
    )(grams[:, cols + bands :])
    return panels, grams[:, : cols + bands].reshape(1, WIDTH, cols + bands), inverse


def sums_by_copies(pix_count, abundance, spectra, support, panel_blocks):
    rows, cols = abundance.shape
    width = cols + spectra.shape[1]
    chunks = rows // (4 * TILE_ROWS)
    share = PANEL // pix_count
    away = pix_count - 1
    dma = pltpu.SemaphoreType.DMA

    def buffer(*shape):
        return pltpu.VMEM(shape, jnp.float32)

    return pl.pallas_call(
        functools.partial(exchange_kernel, pix_count),
        out_shape=(
            jax.ShapeDtypeStruct((rows, WIDTH), jnp.float32),
            jax.ShapeDtypeStruct((pix_count, NPANELS * share, width), jnp.float32),
            jax.ShapeDtypeStruct((WIDTH, WIDTH), jnp.float32),
        ),
        in_specs=[HBM, HBM, SMEM, SMEM],
        out_specs=(HBM, VMEM, VMEM),
        scratch_shapes=[
            buffer(*abundance.shape),
            buffer(*spectra.shape),
            buffer(rows, WIDTH),
            buffer(NPANELS, 2 * chunks, TILE_ROWS, WIDTH),
            buffer(NPANELS, chunks, TILE_ROWS, WIDTH),
            buffer(NPANELS, chunks, TILE_ROWS, WIDTH),
            buffer(NPANELS, chunks, TILE_ROWS, WIDTH),
            buffer(NPANELS, 2 * chunks, TILE_ROWS, WIDTH),
            buffer(PANEL, WIDTH),
            buffer(PANEL, WIDTH),
            buffer(away, share, WIDTH),
            buffer(PANEL, WIDTH),
            buffer(PANEL, WIDTH),
            buffer(away, share, WIDTH),
            buffer(PANEL, width),
            buffer(away, share, width),
            buffer(PANEL, width),
            buffer(away, share, width),
            buffer(PANEL, WIDTH),
            dma((3,)),
            dma,
        ]
        + [dma((NPANELS, chunks))] * 6
        + [dma((4, away)), dma((4, away)), dma((2, away)), dma((2, away)), dma((2, away))],
        compiler_params=pltpu.CompilerParams(
            collective_id=0, has_side_effects=True, vmem_limit_bytes=EXCHANGE_VMEM
        ),
        name="exchange",
    )(abundance, spectra, support, panel_blocks)


def per_device(pix_count, eb_count, abundance, spectra, support, panel_blocks):
    rows, cols = abundance.shape
    bands = spectra.shape[1]
    support = support.T
    args = (abundance, spectra, support, panel_blocks)
    if eb_count == 4 and 1 < pix_count and PANEL % (SUB * pix_count) == 0 and rows % (4 * TILE_ROWS) == 0:
        panels, grams, inverse = sums_by_copies(pix_count, *args)
    else:
        panels, grams, inverse = sums_by_collectives(*args)
    params = pltpu.CompilerParams(vmem_limit_bytes=EXCHANGE_VMEM)
    trailing, residual, coefficients = pl.pallas_call(
        update_kernel,
        out_shape=(
            jax.ShapeDtypeStruct((rows, cols), jnp.float32),
            jax.ShapeDtypeStruct((rows, bands), jnp.float32),
            jax.ShapeDtypeStruct((WIDTH, bands), jnp.float32),
        ),
        in_specs=[HBM, HBM, SMEM, HBM, VMEM, VMEM],
        out_specs=(HBM, HBM, VMEM),
        scratch_shapes=[
            pltpu.VMEM((rows, cols), jnp.float32),
            pltpu.VMEM((rows, bands), jnp.float32),
            pltpu.VMEM((rows, WIDTH), jnp.float32),
            pltpu.VMEM((rows, cols), jnp.float32),
            pltpu.VMEM((rows, bands), jnp.float32),
            pltpu.SemaphoreType.DMA((3,)),
            pltpu.SemaphoreType.DMA((rows // TILE_ROWS,)),
            pltpu.SemaphoreType.DMA((rows // TILE_ROWS,)),
        ],
        compiler_params=params,
        name="update",
    )(abundance, spectra, support, panels, grams, inverse)
    return trailing, residual, coefficients.reshape(NPANELS, PANEL, bands)


def solution(mesh):
    placed = (P("pix", "eb"), P("pix", "eb"), P("pix", "eb"), P())
    return jax.shard_map(
        functools.partial(per_device, mesh.shape["pix"], mesh.shape["eb"]),
        mesh=mesh,
        in_specs=placed,
        out_specs=(P("pix", "eb"), P("pix", "eb"), P(None, None, "eb")),
        check_vma=False,
    )
```

time: 44.8 us -> 41.6 us (0.929)
  local copies, waits for them, and re-layouts: 3.59 us -> 0 us
  Pallas kernels: 40.3 us -> 40.8 us
    unnamed x8 -> x0, local copies, waits for them, and re-layouts: 3.59 us -> none
    pallas_call x1, Pallas kernels: 4.21 us -> 5.31 us  [per_device(): pl.pallas_call(update_kernel, out_shape=(jax.ShapeDtypeStruct((rows, cols...]
    pallas_call x1, Pallas kernels: 36.1 us -> 35.5 us  [sums_by_copies(): pl.pallas_call(functools.partial(exchange_kernel, pix_count), out_shape=(...]
where the time goes in v4:
time: 41.6 us; the launch traced here: 41.4 us
  Pallas kernels  40.8 us (98%)
  between operations  0.64 us (2%)
    pallas_call x1, Pallas kernels, sums_by_copies(): pl.pallas_call(functools.partial(exchange_kernel, pix_count), out_shape=(...  35.5 us
    pallas_call x1, Pallas kernels, per_device(): pl.pallas_call(update_kernel, out_shape=(jax.ShapeDtypeStruct((rows, cols...  5.31 us

profile of v4, /device:TPU:0, one launch (start us, length us, event | category | flops | bytes accessed | tf_op | source)
XLA Modules:
  0.0 41.4 jit_solution(8257916253383658632)
XLA Ops:
  0.6 35.5 %exchange.1 = (f32[1024,128]{1,0:T(8,128)}, f32[8,16,384]{2,1,0:T(8,128)}, f32[128,128]{1,0:T(8,128)}) custom-call(f32[1024,256]{1,0:T(8,128)} %x_hbm.3, f32[1024,128]{1,0:T(8,128)} %y_hbm.3, s32[4,8]{1,0:T(4,128)} %bitcast.2, s32[2]{0:T(128)} %blocks_ref.1), custom_call_target="tpu_custom_call" | custom-call | tf_op jit(solution)/shard_map/exchange/pallas_call | solution.py:492
  36.1 5.3 %update.1 = (f32[1024,256]{1,0:T(8,128)}, f32[1024,128]{1,0:T(8,128)}, f32[128,128]{1,0:T(8,128)}) custom-call(f32[1024,256]{1,0:T(8,128)} %x_hbm.3, f32[1024,128]{1,0:T(8,128)} %y_hbm.3, s32[4,8]{1,0:T(4,128)} %bitcast.3, f32[1024,128]{1,0:T(8,128)} %get-tuple-element.9.c_hbm, f32[8,16,384]{2,1,0:T(8,128)} %get-tuple-element.10.m_ref, ...), custom_call_target="tpu_custom_call" | custom-call | tf_op jit(solution)/shard_map/update/pallas_call | solution.py:543

commit v5 on v4

--- a/solution.py
+++ b/solution.py
@@ -84,10 +84,14 @@
     lax.fori_loop(first, last, step, 0)
 
 
-def inverse_factor(work_ref, gram):
+def start_factor(work_ref, gram):
     row = lax.broadcasted_iota(jnp.int32, (PANEL, PANEL), 0)
     col = lax.broadcasted_iota(jnp.int32, (PANEL, PANEL), 1)
     work_ref[...] = jnp.concatenate([gram, jnp.where(row == col, 1.0, 0.0)], axis=1)
+
+
+def inverse_factor(work_ref, gram):
+    start_factor(work_ref, gram)
     factor_steps(work_ref, 0, PANEL // SUB)
     return work_ref[:, PANEL:]
 
@@ -239,6 +243,8 @@
     m0_sems,
     m1_sems,
     gather_sems,
+    near0_sems,
+    near1_sems,
 ):
     rows, cols = x_ref.shape
     half = rows // 2
@@ -266,7 +272,8 @@
         loads[-1].start()
 
     barrier = pltpu.get_barrier_semaphore()
-    for target in [(pix, beside), (pix, across)] + [(other, eb) for other in others]:
+    near = [(pix, (eb + d) % 4) for d in range(1, 4)]
+    for target in near + [(other, eb) for other in others]:
         pl.semaphore_signal(barrier, inc=1, device_id=target, device_id_type=pl.DeviceIdType.MESH)
 
     started = []
@@ -303,17 +310,11 @@
         value = product_t(panel, c_ref[pair_span(pair), :])
         part[...] = value if first else part[...] + value
 
-    def add_products(index, part):
-        total = None
-        for pair in range(2 * chunks):
-            panel = c_ref[pair * 2 * TILE_ROWS : (pair + 1) * 2 * TILE_ROWS, index * PANEL : (index + 1) * PANEL]
-            masked = jnp.concatenate(
-                [masked_tile(x_ref, support_ref, pair * 2 + place) for place in range(2)], axis=0
-            )
-            values = y_ref[pair * 2 * TILE_ROWS : (pair + 1) * 2 * TILE_ROWS, :]
-            value = product_t(panel, jnp.concatenate([masked, values], axis=1))
-            total = value if total is None else total + value
-        part[...] = total
+    def add_products(index, pair, part, first):
+        panel = c_ref[pair_span(pair), index * PANEL : (index + 1) * PANEL]
+        masked = jnp.concatenate([masked_tile(x_ref, support_ref, pair * 2 + place) for place in range(2)], axis=0)
+        value = product_t(panel, jnp.concatenate([masked, y_ref[pair_span(pair), :]], axis=1))
+        part[...] = value if first else part[...] + value
 
     share = PANEL // pix_count
     mine = pl.ds(pl.multiple_of(pix * share, share), share)
@@ -340,8 +341,27 @@
             for index, other in enumerate(others)
         ]
 
-    def arrive(index):
-        part = gram0_part if index == 0 else gram1_part
+    quarter = PANEL // 4
+    here = pl.ds(pl.multiple_of(eb * quarter, quarter), quarter)
+
+    def spread_gram(part, landing, sems):
+        return [
+            send(part.at[here, :], landing.at[index], sems.at[0, index], sems.at[1, index], (other, eb))
+            for index, other in enumerate(others)
+        ]
+
+    def share_gram(part, landing, gram, copies, sems):
+        total = part[here, :]
+        for index in range(pix_count - 1):
+            copies[index].wait_recv()
+            total = total + landing[index]
+        gram[here, :] = total
+        return [
+            send(gram.at[here, :], gram.at[here, :], sems.at[0, index], sems.at[1, index], target)
+            for index, target in enumerate(near)
+        ]
+
+    def arrive(index, part):
         copies3 = []
         for chunk in range(chunks):
             copies2[index][chunk].wait_recv()
@@ -368,7 +388,7 @@
     loads[0].wait()
     for chunk in range(chunks):
         prepare(other_core, chunk)
-    pl.semaphore_wait(barrier, pix_count + 1)
+    pl.semaphore_wait(barrier, pix_count + 2)
     copies1 = [
         [
             send(
@@ -402,32 +422,40 @@
             )
     loads[2].wait()
 
-    arrive(0)
-    gram0_copies = scatter(gram0_part, gram0_slots, gram0_sems)
-    add_products(0, m0_part)
-    gram0[mine, :] = add_up(gram0_part, gram0_slots, gram0_copies)
-    gram0_gather = gather(gram0.at[mine, :], gram0_sems, 2)
+    low_rows = pl.ds(0, share)
+    high_rows = pl.ds(share, share)
+    steps = PANEL // SUB
+
+    arrive(0, gram0_part)
+    gram0_copies = spread_gram(gram0_part, gram0_slots, gram0_sems)
+    for pair in range(2 * chunks):
+        add_products(0, pair, m0_part, pair == 0)
     m0_copies = scatter(m0_part, m0_slots, m0_sems)
-
-    arrive(1)
-    gram1_copies = scatter(gram1_part, gram1_slots, gram1_sems)
+    gram0_near = share_gram(gram0_part, gram0_slots, gram0, gram0_copies, near0_sems)
+
+    arrive(1, gram1_part)
+    gram1_copies = spread_gram(gram1_part, gram1_slots, gram1_sems)
+    for pair in range(2 * chunks):
+        add_products(1, pair, m1_part, pair == 0)
+    m1_copies = scatter(m1_part, m1_slots, m1_sems)
     keep_c = pltpu.make_async_copy(c_ref, c_hbm, out_sem)
     keep_c.start()
-    add_products(1, m1_part)
-    gram1[mine, :] = add_up(gram1_part, gram1_slots, gram1_copies)
-    gram1_gather = gather(gram1.at[mine, :], gram1_sems, 2)
-    m1_copies = scatter(m1_part, m1_slots, m1_sems)
-
-    for copy in gram0_gather:
+    m_ref[pix, low_rows, :] = add_up(m0_part, m0_slots, m0_copies)
+    m0_gather = gather(m_ref.at[pix, low_rows, :], gather_sems, 0)
+
+    for copy in gram0_near:
         copy.wait_recv()
-    inverse0 = inverse_factor(work_ref, gram0[:, :PANEL])
-    m_ref[pix, :share, :] = add_up(m0_part, m0_slots, m0_copies)
-    m_ref[pix, share:, :] = add_up(m1_part, m1_slots, m1_copies)
-    m_gather = gather(m_ref.at[pix], gather_sems, 0)
-    for copy in gram1_gather:
+    start_factor(work_ref, gram0[:, :PANEL])
+    factor_steps(work_ref, 0, steps // 2)
+    gram1_near = share_gram(gram1_part, gram1_slots, gram1, gram1_copies, near1_sems)
+    factor_steps(work_ref, steps // 2, steps)
+    inverse0 = work_ref[:, PANEL:]
+    m_ref[pix, high_rows, :] = add_up(m1_part, m1_slots, m1_copies)
+    m1_gather = gather(m_ref.at[pix, high_rows, :], gather_sems, 2)
+    for copy in gram1_near:
         copy.wait_recv()
     second_factor(work_ref, inverse0, gram1[...], inverse_ref)
-    for copy in m_gather:
+    for copy in m0_gather + m1_gather:
         copy.wait_recv()
     for copy in started:
         copy.wait_send()
@@ -509,10 +537,10 @@
             buffer(NPANELS, 2 * chunks, TILE_ROWS, WIDTH),
             buffer(PANEL, WIDTH),
             buffer(PANEL, WIDTH),
-            buffer(away, share, WIDTH),
+            buffer(away, PANEL // 4, WIDTH),
             buffer(PANEL, WIDTH),
             buffer(PANEL, WIDTH),
-            buffer(away, share, WIDTH),
+            buffer(away, PANEL // 4, WIDTH),
             buffer(PANEL, width),
             buffer(away, share, width),
             buffer(PANEL, width),
@@ -522,7 +550,8 @@
             dma,
         ]
         + [dma((NPANELS, chunks))] * 6
-        + [dma((4, away)), dma((4, away)), dma((2, away)), dma((2, away)), dma((2, away))],
+        + [dma((2, away))] * 4
+        + [dma((4, away)), dma((2, 3)), dma((2, 3))],
         compiler_params=pltpu.CompilerParams(
             collective_id=0, has_side_effects=True, vmem_limit_bytes=EXCHANGE_VMEM
         ),

time: 41.6 us -> 39.9 us (0.959)
  Pallas kernels: 40.8 us -> 39 us
    pallas_call x1, Pallas kernels: 35.5 us -> 33.7 us  [sums_by_copies(): pl.pallas_call(functools.partial(exchange_kernel, pix_count), out_shape=(...]
where the time goes in v5:
time: 39.9 us; the launch traced here: 39.7 us
  Pallas kernels  39 us (98%)
  between operations  0.64 us (2%)
    pallas_call x1, Pallas kernels, sums_by_copies(): pl.pallas_call(functools.partial(exchange_kernel, pix_count), out_shape=(...  33.7 us
    pallas_call x1, Pallas kernels, per_device(): pl.pallas_call(update_kernel, out_shape=(jax.ShapeDtypeStruct((rows, cols...  5.3 us

profile of v5, /device:TPU:0, one launch (start us, length us, event | category | flops | bytes accessed | tf_op | source)
XLA Modules:
  0.0 39.7 jit_solution(7571026405431126486)
XLA Ops:
  0.6 33.7 %exchange.1 = (f32[1024,128]{1,0:T(8,128)}, f32[8,16,384]{2,1,0:T(8,128)}, f32[128,128]{1,0:T(8,128)}) custom-call(f32[1024,256]{1,0:T(8,128)} %x_hbm.3, f32[1024,128]{1,0:T(8,128)} %y_hbm.3, s32[4,8]{1,0:T(4,128)} %bitcast.2, s32[2]{0:T(128)} %blocks_ref.1), custom_call_target="tpu_custom_call" | custom-call | tf_op jit(solution)/shard_map/exchange/pallas_call | solution.py:520
  34.4 5.3 %update.1 = (f32[1024,256]{1,0:T(8,128)}, f32[1024,128]{1,0:T(8,128)}, f32[128,128]{1,0:T(8,128)}) custom-call(f32[1024,256]{1,0:T(8,128)} %x_hbm.3, f32[1024,128]{1,0:T(8,128)} %y_hbm.3, s32[4,8]{1,0:T(4,128)} %bitcast.3, f32[1024,128]{1,0:T(8,128)} %get-tuple-element.9.c_hbm, f32[8,16,384]{2,1,0:T(8,128)} %get-tuple-element.10.m_ref, ...), custom_call_target="tpu_custom_call" | custom-call | tf_op jit(solution)/shard_map/update/pallas_call | solution.py:572

commit v6 on v5

--- a/solution.py
+++ b/solution.py
@@ -30,6 +30,15 @@
     )
 
 
+def split(values):
+    high = values.astype(jnp.bfloat16)
+    return high, (values - high.astype(jnp.float32)).astype(jnp.bfloat16)
+
+
+def plain(left, right):
+    return jnp.dot(left, right, preferred_element_type=jnp.float32)
+
+
 def product_nt(left, right):
     return lax.dot_general(
         left,
@@ -49,16 +58,25 @@
     return row
 
 
-def factor_steps(work_ref, first, last):
+def inverse_factor(gram):
     shape = (SUB, WIDTH)
-
-    def step(block, carry):
-        sublane = lax.broadcasted_iota(jnp.int32, shape, 0)
-        row = lax.broadcasted_iota(jnp.int32, (PANEL, SUB), 0)
-        low = pl.multiple_of(block * SUB, SUB)
-        rows = work_ref[pl.ds(low, SUB), :]
-        turned = pltpu.roll(rows, (WIDTH - low) % WIDTH, 1)
-        columns = [jnp.broadcast_to(turned[:, j : j + 1], shape) for j in range(SUB)]
+    count = PANEL // SUB
+    sublane = lax.broadcasted_iota(jnp.int32, shape, 0)
+    lane = lax.broadcasted_iota(jnp.int32, shape, 1)
+    pad = jnp.concatenate([gram, jnp.zeros_like(gram)], axis=1)
+    tiles = [
+        pad[i * SUB : (i + 1) * SUB, :] + jnp.where(lane == sublane + (PANEL + i * SUB), 1.0, 0.0)
+        for i in range(count)
+    ]
+    for block in range(count):
+        low = block * SUB
+
+        def spread(tile):
+            return [jnp.broadcast_to(tile[:, low + j : low + j + 1], shape) for j in range(SUB)]
+
+        rows = tiles[block]
+        columns = spread(rows)
+        below = {r: spread(tiles[r]) for r in range(block + 1, count)}
         entry = {
             (i, j): jnp.broadcast_to(columns[j][i : i + 1, :], shape)
             for j in range(SUB)
@@ -76,32 +94,21 @@
                     entry[i, k] = entry[i, k] - entry[i, j] * entry[k, j]
                 g[i] = g[i] - entry[i, j] * g[j]
             upper = jnp.where(sublane == j, g[j], upper)
-        below = jnp.where(row >= low + SUB, upper.T[:PANEL, :], 0.0)
-        work_ref[...] = work_ref[...] - product(below, upper)
-        work_ref[pl.ds(low, SUB), :] = upper
-        return carry
-
-    lax.fori_loop(first, last, step, 0)
-
-
-def start_factor(work_ref, gram):
-    row = lax.broadcasted_iota(jnp.int32, (PANEL, PANEL), 0)
-    col = lax.broadcasted_iota(jnp.int32, (PANEL, PANEL), 1)
-    work_ref[...] = jnp.concatenate([gram, jnp.where(row == col, 1.0, 0.0)], axis=1)
-
-
-def inverse_factor(work_ref, gram):
-    start_factor(work_ref, gram)
-    factor_steps(work_ref, 0, PANEL // SUB)
-    return work_ref[:, PANEL:]
-
-
-def second_factor(work_ref, inverse0, grams1, inverse_ref):
+            for r, column in below.items():
+                column[j] = column[j] * scale
+                for k in range(j + 1, SUB):
+                    column[k] = column[k] - column[j] * entry[k, j]
+                tiles[r] = tiles[r] - column[j] * g[j]
+        tiles[block] = upper
+    return jnp.concatenate(tiles, axis=0)[:, PANEL:]
+
+
+def second_factor(inverse0, grams1, inverse_ref):
     coupling = product_nt(grams1[:, :PANEL], inverse0)
     remainder = grams1[:, PANEL:] - product_nt(coupling, coupling)
     carried = product(coupling, inverse0)
     inverse_ref[:PANEL, :] = jnp.concatenate([inverse0, jnp.zeros_like(inverse0)], axis=1)
-    inverse1 = inverse_factor(work_ref, remainder)
+    inverse1 = inverse_factor(remainder)
     inverse_ref[PANEL:, :] = jnp.concatenate([-product(inverse1, carried), inverse1], axis=1)
 
 
@@ -117,9 +124,9 @@
     out_ref[...] = total
 
 
-def factor_kernel(gram_ref, inverse_ref, work_ref):
-    inverse0 = inverse_factor(work_ref, gram_ref[:PANEL, :PANEL])
-    second_factor(work_ref, inverse0, gram_ref[PANEL:, :], inverse_ref)
+def factor_kernel(gram_ref, inverse_ref):
+    inverse0 = inverse_factor(gram_ref[:PANEL, :PANEL])
+    second_factor(inverse0, gram_ref[PANEL:, :], inverse_ref)
 
 
 def update_kernel(
@@ -156,13 +163,15 @@
     )
     proj = product(inverse, sums)
     coef_ref[...] = proj[:, cols:]
-    weights = product_t(inverse, proj)
+    high, low = split(product_t(inverse, proj))
+    weights = jnp.concatenate([high, high, low], axis=0)
     for copy in loads:
         copy.wait()
     stores = []
     for tile in range(rows // TILE_ROWS):
         span = pl.ds(tile * TILE_ROWS, TILE_ROWS)
-        change = product(c_ref[span, :], weights)
+        high, low = split(c_ref[span, :])
+        change = plain(jnp.concatenate([high, low, high], axis=1), weights)
         trail[span, :] = masked_tile(x_ref, support_ref, tile) - change[:, :cols]
         resid[span, :] = y_ref[span, :] - change[:, cols:]
         stores.append(pltpu.make_async_copy(trail.at[span, :], trail_hbm.at[span, :], trail_sem.at[tile]))
@@ -229,7 +238,8 @@
     m0_slots,
     m1_part,
     m1_slots,
-    work_ref,
+    xy_high,
+    xy_low,
     in_sem,
     out_sem,
     send1,
@@ -312,8 +322,9 @@
 
     def add_products(index, pair, part, first):
         panel = c_ref[pair_span(pair), index * PANEL : (index + 1) * PANEL]
-        masked = jnp.concatenate([masked_tile(x_ref, support_ref, pair * 2 + place) for place in range(2)], axis=0)
-        value = product_t(panel, jnp.concatenate([masked, y_ref[pair_span(pair), :]], axis=1))
+        high, low = split(panel.T)
+        both = plain(jnp.concatenate([high, low], axis=0), xy_high[pair_span(pair), :])
+        value = both[:PANEL] + both[PANEL:] + plain(high, xy_low[pair_span(pair), :])
         part[...] = value if first else part[...] + value
 
     share = PANEL // pix_count
@@ -421,10 +432,17 @@
                 )
             )
     loads[2].wait()
+    for tile in range(rows // TILE_ROWS):
+        for values, lanes in [
+            (masked_tile(x_ref, support_ref, tile), slice(0, cols)),
+            (y_ref[tile_span(tile), :], slice(cols, None)),
+        ]:
+            high, low = split(values)
+            xy_high[tile_span(tile), lanes] = high
+            xy_low[tile_span(tile), lanes] = low
 
     low_rows = pl.ds(0, share)
     high_rows = pl.ds(share, share)
-    steps = PANEL // SUB
 
     arrive(0, gram0_part)
     gram0_copies = spread_gram(gram0_part, gram0_slots, gram0_sems)
@@ -445,16 +463,13 @@
 
     for copy in gram0_near:
         copy.wait_recv()
-    start_factor(work_ref, gram0[:, :PANEL])
-    factor_steps(work_ref, 0, steps // 2)
+    inverse0 = inverse_factor(gram0[:, :PANEL])
     gram1_near = share_gram(gram1_part, gram1_slots, gram1, gram1_copies, near1_sems)
-    factor_steps(work_ref, steps // 2, steps)
-    inverse0 = work_ref[:, PANEL:]
     m_ref[pix, high_rows, :] = add_up(m1_part, m1_slots, m1_copies)
     m1_gather = gather(m_ref.at[pix, high_rows, :], gather_sems, 2)
     for copy in gram1_near:
         copy.wait_recv()
-    second_factor(work_ref, inverse0, gram1[...], inverse_ref)
+    second_factor(inverse0, gram1[...], inverse_ref)
     for copy in m0_gather + m1_gather:
         copy.wait_recv()
     for copy in started:
@@ -499,7 +514,6 @@
         out_shape=jax.ShapeDtypeStruct((WIDTH, WIDTH), jnp.float32),
         in_specs=[VMEM],
         out_specs=VMEM,
-        scratch_shapes=[pltpu.VMEM((PANEL, WIDTH), jnp.float32)],
         compiler_params=pltpu.CompilerParams(vmem_limit_bytes=VMEM_LIMIT),
         name="factor",
     )(grams[:, cols + bands :])
@@ -545,7 +559,8 @@
             buffer(away, share, width),
             buffer(PANEL, width),
             buffer(away, share, width),
-            buffer(PANEL, WIDTH),
+            pltpu.VMEM((rows, width), jnp.bfloat16),
+            pltpu.VMEM((rows, width), jnp.bfloat16),
             dma((3,)),
             dma,
         ]

time: 39.9 us -> 39.1 us (0.980)
  Pallas kernels: 39 us -> 38.2 us
    pallas_call x1, Pallas kernels: 5.3 us -> 4.61 us  [per_device(): pl.pallas_call(update_kernel, out_shape=(jax.ShapeDtypeStruct((rows, cols...]
where the time goes in v6:
time: 39.1 us; the launch traced here: 38.8 us
  Pallas kernels  38.2 us (98%)
  between operations  0.64 us (2%)
    pallas_call x1, Pallas kernels, sums_by_copies(): pl.pallas_call(functools.partial(exchange_kernel, pix_count), out_shape=(...  33.6 us
    pallas_call x1, Pallas kernels, per_device(): pl.pallas_call(update_kernel, out_shape=(jax.ShapeDtypeStruct((rows, cols...  4.61 us

profile of v6, /device:TPU:0, one launch (start us, length us, event | category | flops | bytes accessed | tf_op | source)
XLA Modules:
  0.0 38.8 jit_solution(2874483040607527163)
XLA Ops:
  0.6 33.6 %exchange.1 = (f32[1024,128]{1,0:T(8,128)}, f32[8,16,384]{2,1,0:T(8,128)}, f32[128,128]{1,0:T(8,128)}) custom-call(f32[1024,256]{1,0:T(8,128)} %x_hbm.3, f32[1024,128]{1,0:T(8,128)} %y_hbm.3, s32[4,8]{1,0:T(4,128)} %bitcast.2, s32[2]{0:T(128)} %blocks_ref.1), custom_call_target="tpu_custom_call" | custom-call | tf_op jit(solution)/shard_map/exchange/pallas_call | solution.py:534
  34.2 4.6 %update.1 = (f32[1024,256]{1,0:T(8,128)}, f32[1024,128]{1,0:T(8,128)}, f32[128,128]{1,0:T(8,128)}) custom-call(f32[1024,256]{1,0:T(8,128)} %x_hbm.3, f32[1024,128]{1,0:T(8,128)} %y_hbm.3, s32[4,8]{1,0:T(4,128)} %bitcast.3, f32[1024,128]{1,0:T(8,128)} %get-tuple-element.9.c_hbm, f32[8,16,384]{2,1,0:T(8,128)} %get-tuple-element.10.m_ref, ...), custom_call_target="tpu_custom_call" | custom-call | tf_op jit(solution)/shard_map/update/pallas_call | solution.py:587

commit v7 on v6

--- a/solution.py
+++ b/solution.py
@@ -134,40 +134,44 @@
     y_hbm,
     support_ref,
     c_hbm,
-    m_ref,
-    inverse_ref,
+    m_hbm,
+    inverse_hbm,
     trail_hbm,
     resid_hbm,
-    coef_ref,
+    coef_hbm,
     x_ref,
     y_ref,
     c_ref,
+    m_ref,
+    inverse_ref,
+    coef,
     trail,
     resid,
     in_sem,
     trail_sem,
     resid_sem,
+    coef_sem,
 ):
     rows, cols = x_ref.shape
-    loads = [
-        pltpu.make_async_copy(x_hbm, x_ref, in_sem.at[0]),
-        pltpu.make_async_copy(y_hbm, y_ref, in_sem.at[1]),
-        pltpu.make_async_copy(c_hbm, c_ref, in_sem.at[2]),
-    ]
+    pairs = [(inverse_hbm, inverse_ref), (m_hbm, m_ref), (c_hbm, c_ref), (x_hbm, x_ref), (y_hbm, y_ref)]
+    loads = [pltpu.make_async_copy(src, dst, in_sem.at[index]) for index, (src, dst) in enumerate(pairs)]
     for copy in loads:
         copy.start()
+    for copy in loads[:2]:
+        copy.wait()
     inverse = inverse_ref[...]
     share = m_ref.shape[1] // NPANELS
     sums = jnp.concatenate(
         [m_ref[p, i * share : (i + 1) * share, :] for i in range(NPANELS) for p in range(m_ref.shape[0])], axis=0
     )
     proj = product(inverse, sums)
-    coef_ref[...] = proj[:, cols:]
+    coef[...] = proj[:, cols:]
+    stores = [pltpu.make_async_copy(coef, coef_hbm, coef_sem)]
+    stores[0].start()
     high, low = split(product_t(inverse, proj))
     weights = jnp.concatenate([high, high, low], axis=0)
-    for copy in loads:
+    for copy in loads[2:]:
         copy.wait()
-    stores = []
     for tile in range(rows // TILE_ROWS):
         span = pl.ds(tile * TILE_ROWS, TILE_ROWS)
         high, low = split(c_ref[span, :])
@@ -315,10 +319,8 @@
         c_ref[tile_span(pair * 2), lanes] = packed[:, :PANEL]
         c_ref[tile_span(pair * 2 + 1), lanes] = packed[:, PANEL:]
 
-    def add_gram(index, pair, part, first):
-        panel = c_ref[pair_span(pair), index * PANEL : (index + 1) * PANEL]
-        value = product_t(panel, c_ref[pair_span(pair), :])
-        part[...] = value if first else part[...] + value
+    def gram_of(index):
+        return product_t(c_ref[:, index * PANEL : (index + 1) * PANEL], c_ref[...])
 
     def add_products(index, pair, part, first):
         panel = c_ref[pair_span(pair), index * PANEL : (index + 1) * PANEL]
@@ -388,12 +390,12 @@
                 )
             )
             unpack(index, pair)
-            add_gram(index, pair, part, chunk == 0)
+            add_products(index, pair, part, chunk == 0)
         for chunk in range(chunks):
             copies3[chunk].wait_recv()
             pair = other_core * chunks + chunk
             unpack(index, pair)
-            add_gram(index, pair, part, False)
+            add_products(index, pair, part, False)
 
     c_ref[...] = jnp.zeros_like(c_ref)
     loads[0].wait()
@@ -444,18 +446,16 @@
     low_rows = pl.ds(0, share)
     high_rows = pl.ds(share, share)
 
-    arrive(0, gram0_part)
+    arrive(0, m0_part)
+    m0_copies = scatter(m0_part, m0_slots, m0_sems)
+    gram0_part[...] = gram_of(0)
     gram0_copies = spread_gram(gram0_part, gram0_slots, gram0_sems)
-    for pair in range(2 * chunks):
-        add_products(0, pair, m0_part, pair == 0)
-    m0_copies = scatter(m0_part, m0_slots, m0_sems)
+
+    arrive(1, m1_part)
+    m1_copies = scatter(m1_part, m1_slots, m1_sems)
     gram0_near = share_gram(gram0_part, gram0_slots, gram0, gram0_copies, near0_sems)
-
-    arrive(1, gram1_part)
+    gram1_part[...] = gram_of(1)
     gram1_copies = spread_gram(gram1_part, gram1_slots, gram1_sems)
-    for pair in range(2 * chunks):
-        add_products(1, pair, m1_part, pair == 0)
-    m1_copies = scatter(m1_part, m1_slots, m1_sems)
     keep_c = pltpu.make_async_copy(c_ref, c_hbm, out_sem)
     keep_c.start()
     m_ref[pix, low_rows, :] = add_up(m0_part, m0_slots, m0_copies)
@@ -591,17 +591,21 @@
             jax.ShapeDtypeStruct((rows, bands), jnp.float32),
             jax.ShapeDtypeStruct((WIDTH, bands), jnp.float32),
         ),
-        in_specs=[HBM, HBM, SMEM, HBM, VMEM, VMEM],
-        out_specs=(HBM, HBM, VMEM),
+        in_specs=[HBM, HBM, SMEM, HBM, HBM, HBM],
+        out_specs=(HBM, HBM, HBM),
         scratch_shapes=[
             pltpu.VMEM((rows, cols), jnp.float32),
             pltpu.VMEM((rows, bands), jnp.float32),
             pltpu.VMEM((rows, WIDTH), jnp.float32),
+            pltpu.VMEM(grams.shape, jnp.float32),
+            pltpu.VMEM((WIDTH, WIDTH), jnp.float32),
+            pltpu.VMEM((WIDTH, bands), jnp.float32),
             pltpu.VMEM((rows, cols), jnp.float32),
             pltpu.VMEM((rows, bands), jnp.float32),
-            pltpu.SemaphoreType.DMA((3,)),
+            pltpu.SemaphoreType.DMA((5,)),
             pltpu.SemaphoreType.DMA((rows // TILE_ROWS,)),
             pltpu.SemaphoreType.DMA((rows // TILE_ROWS,)),
+            pltpu.SemaphoreType.DMA,
         ],
         compiler_params=params,
         name="update",

time: 39.1 us -> 36.6 us (0.936)
  Pallas kernels: 38.2 us -> 35.8 us
    pallas_call x1, Pallas kernels: 33.6 us -> 31.9 us  [sums_by_copies(): pl.pallas_call(functools.partial(exchange_kernel, pix_count), out_shape=(...]
    pallas_call x1, Pallas kernels: 4.61 us -> 3.89 us  [per_device(): pl.pallas_call(update_kernel, out_shape=(jax.ShapeDtypeStruct((rows, cols...]
where the time goes in v7:
time: 36.6 us; the launch traced here: 36.4 us
  Pallas kernels  35.8 us (98%)
  between operations  0.64 us (2%)
    pallas_call x1, Pallas kernels, sums_by_copies(): pl.pallas_call(functools.partial(exchange_kernel, pix_count), out_shape=(...  31.9 us
    pallas_call x1, Pallas kernels, per_device(): pl.pallas_call(update_kernel, out_shape=(jax.ShapeDtypeStruct((rows, cols...  3.89 us

profile of v7, /device:TPU:0, one launch (start us, length us, event | category | flops | bytes accessed | tf_op | source)
XLA Modules:
  0.0 36.4 jit_solution(13893653586745977562)
XLA Ops:
  0.6 31.9 %exchange.1 = (f32[1024,128]{1,0:T(8,128)}, f32[8,16,384]{2,1,0:T(8,128)}, f32[128,128]{1,0:T(8,128)}) custom-call(f32[1024,256]{1,0:T(8,128)} %x_hbm.3, f32[1024,128]{1,0:T(8,128)} %y_hbm.3, s32[4,8]{1,0:T(4,128)} %bitcast.2, s32[2]{0:T(128)} %blocks_ref.1), custom_call_target="tpu_custom_call" | custom-call | tf_op jit(solution)/shard_map/exchange/pallas_call | solution.py:534
  32.5 3.9 %update.1 = (f32[1024,256]{1,0:T(8,128)}, f32[1024,128]{1,0:T(8,128)}, f32[128,128]{1,0:T(8,128)}) custom-call(f32[1024,256]{1,0:T(8,128)} %x_hbm.3, f32[1024,128]{1,0:T(8,128)} %y_hbm.3, s32[4,8]{1,0:T(4,128)} %bitcast.3, f32[1024,128]{1,0:T(8,128)} %get-tuple-element.9.c_hbm, f32[8,16,384]{2,1,0:T(8,128)} %get-tuple-element.10.m_hbm, ...), custom_call_target="tpu_custom_call" | custom-call | tf_op jit(solution)/shard_map/update/pallas_call | solution.py:587

commit v8 on v7

--- a/solution.py
+++ b/solution.py
@@ -219,13 +219,15 @@
     pix_count,
     x_hbm,
     y_hbm,
-    support_ref,
-    blocks_ref,
+    support_hbm,
+    blocks_hbm,
     c_hbm,
     m_ref,
     inverse_ref,
     x_ref,
     y_ref,
+    support_ref,
+    blocks_ref,
     c_ref,
     own,
     first_in,
@@ -280,6 +282,8 @@
             (side_of(x_hbm, other_core), side_of(x_ref, other_core)),
             (side_of(x_hbm, core), side_of(x_ref, core)),
             (y_hbm, y_ref),
+            (support_hbm, support_ref),
+            (blocks_hbm, blocks_ref),
         ]
     ):
         loads.append(pltpu.make_async_copy(src, dst, in_sem.at[index]))
@@ -398,6 +402,8 @@
             add_products(index, pair, part, False)
 
     c_ref[...] = jnp.zeros_like(c_ref)
+    loads[3].wait()
+    loads[4].wait()
     loads[0].wait()
     for chunk in range(chunks):
         prepare(other_core, chunk)
@@ -470,11 +476,13 @@
     for copy in gram1_near:
         copy.wait_recv()
     second_factor(inverse0, gram1[...], inverse_ref)
+    for copy in started[: -len(m1_gather)]:
+        copy.wait_send()
+    keep_c.wait()
     for copy in m0_gather + m1_gather:
         copy.wait_recv()
-    for copy in started:
+    for copy in m1_gather:
         copy.wait_send()
-    keep_c.wait()
 
 
 VMEM = pl.BlockSpec(memory_space=pltpu.VMEM)
@@ -538,11 +546,13 @@
             jax.ShapeDtypeStruct((pix_count, NPANELS * share, width), jnp.float32),
             jax.ShapeDtypeStruct((WIDTH, WIDTH), jnp.float32),
         ),
-        in_specs=[HBM, HBM, SMEM, SMEM],
+        in_specs=[HBM, HBM, HBM, HBM],
         out_specs=(HBM, VMEM, VMEM),
         scratch_shapes=[
             buffer(*abundance.shape),
             buffer(*spectra.shape),
+            pltpu.SMEM(support.shape, jnp.int32),
+            pltpu.SMEM(panel_blocks.shape, jnp.int32),
             buffer(rows, WIDTH),
             buffer(NPANELS, 2 * chunks, TILE_ROWS, WIDTH),
             buffer(NPANELS, chunks, TILE_ROWS, WIDTH),
@@ -561,7 +571,7 @@
             buffer(away, share, width),
             pltpu.VMEM((rows, width), jnp.bfloat16),
             pltpu.VMEM((rows, width), jnp.bfloat16),
-            dma((3,)),
+            dma((5,)),
             dma,
         ]
         + [dma((NPANELS, chunks))] * 6

time: 36.6 us -> 35.9 us (0.981)
  Pallas kernels: 35.8 us -> 35.1 us
    pallas_call x1, Pallas kernels: 31.9 us -> 31.2 us  [sums_by_copies(): pl.pallas_call(functools.partial(exchange_kernel, pix_count), out_shape=(...]
where the time goes in v8:
time: 35.9 us; the launch traced here: 35.7 us
  Pallas kernels  35.1 us (98%)
  between operations  0.64 us (2%)
    pallas_call x1, Pallas kernels, sums_by_copies(): pl.pallas_call(functools.partial(exchange_kernel, pix_count), out_shape=(...  31.2 us
    pallas_call x1, Pallas kernels, per_device(): pl.pallas_call(update_kernel, out_shape=(jax.ShapeDtypeStruct((rows, cols...  3.89 us

profile of v8, /device:TPU:0, one launch (start us, length us, event | category | flops | bytes accessed | tf_op | source)
XLA Modules:
  0.0 35.7 jit_solution(2021483015503633940)
XLA Ops:
  0.6 31.2 %exchange.1 = (f32[1024,128]{1,0:T(8,128)}, f32[8,16,384]{2,1,0:T(8,128)}, f32[128,128]{1,0:T(8,128)}) custom-call(f32[1024,256]{1,0:T(8,128)} %x_hbm.3, f32[1024,128]{1,0:T(8,128)} %y_hbm.3, s32[4,8]{1,0:T(4,128)} %bitcast.2, s32[2]{0:T(128)} %blocks_hbm.1), custom_call_target="tpu_custom_call" | custom-call | tf_op jit(solution)/shard_map/exchange/pallas_call | solution.py:542
  31.8 3.9 %update.1 = (f32[1024,256]{1,0:T(8,128)}, f32[1024,128]{1,0:T(8,128)}, f32[128,128]{1,0:T(8,128)}) custom-call(f32[1024,256]{1,0:T(8,128)} %x_hbm.3, f32[1024,128]{1,0:T(8,128)} %y_hbm.3, s32[4,8]{1,0:T(4,128)} %bitcast.3, f32[1024,128]{1,0:T(8,128)} %get-tuple-element.9.c_hbm, f32[8,16,384]{2,1,0:T(8,128)} %get-tuple-element.10.m_hbm, ...), custom_call_target="tpu_custom_call" | custom-call | tf_op jit(solution)/shard_map/update/pallas_call | solution.py:597

commit v9 on v8

--- a/solution.py
+++ b/solution.py
@@ -132,7 +132,7 @@
 def update_kernel(
     x_hbm,
     y_hbm,
-    support_ref,
+    support_hbm,
     c_hbm,
     m_hbm,
     inverse_hbm,
@@ -141,6 +141,7 @@
     coef_hbm,
     x_ref,
     y_ref,
+    support_ref,
     c_ref,
     m_ref,
     inverse_ref,
@@ -154,6 +155,7 @@
 ):
     rows, cols = x_ref.shape
     pairs = [(inverse_hbm, inverse_ref), (m_hbm, m_ref), (c_hbm, c_ref), (x_hbm, x_ref), (y_hbm, y_ref)]
+    pairs.append((support_hbm, support_ref))
     loads = [pltpu.make_async_copy(src, dst, in_sem.at[index]) for index, (src, dst) in enumerate(pairs)]
     for copy in loads:
         copy.start()
@@ -601,18 +603,19 @@
             jax.ShapeDtypeStruct((rows, bands), jnp.float32),
             jax.ShapeDtypeStruct((WIDTH, bands), jnp.float32),
         ),
-        in_specs=[HBM, HBM, SMEM, HBM, HBM, HBM],
+        in_specs=[HBM] * 6,
         out_specs=(HBM, HBM, HBM),
         scratch_shapes=[
             pltpu.VMEM((rows, cols), jnp.float32),
             pltpu.VMEM((rows, bands), jnp.float32),
+            pltpu.SMEM(support.shape, jnp.int32),
             pltpu.VMEM((rows, WIDTH), jnp.float32),
             pltpu.VMEM(grams.shape, jnp.float32),
             pltpu.VMEM((WIDTH, WIDTH), jnp.float32),
             pltpu.VMEM((WIDTH, bands), jnp.float32),
             pltpu.VMEM((rows, cols), jnp.float32),
             pltpu.VMEM((rows, bands), jnp.float32),
-            pltpu.SemaphoreType.DMA((5,)),
+            pltpu.SemaphoreType.DMA((6,)),
             pltpu.SemaphoreType.DMA((rows // TILE_ROWS,)),
             pltpu.SemaphoreType.DMA((rows // TILE_ROWS,)),
             pltpu.SemaphoreType.DMA,

time: 35.9 us -> 35.2 us (0.981)
  Pallas kernels: 35.1 us -> 34.4 us
    pallas_call x1, Pallas kernels: 3.89 us -> 3.22 us  [per_device(): pl.pallas_call(update_kernel, out_shape=(jax.ShapeDtypeStruct((rows, cols...]
where the time goes in v9:
time: 35.2 us; the launch traced here: 35.1 us
  Pallas kernels  34.4 us (98%)
  between operations  0.64 us (2%)
    pallas_call x1, Pallas kernels, sums_by_copies(): pl.pallas_call(functools.partial(exchange_kernel, pix_count), out_shape=(...  31.2 us
    pallas_call x1, Pallas kernels, per_device(): pl.pallas_call(update_kernel, out_shape=(jax.ShapeDtypeStruct((rows, cols...  3.22 us

profile of v9, /device:TPU:0, one launch (start us, length us, event | category | flops | bytes accessed | tf_op | source)
XLA Modules:
  0.0 35.1 jit_solution(3507344375857759936)
XLA Ops:
  0.6 31.2 %exchange.1 = (f32[1024,128]{1,0:T(8,128)}, f32[8,16,384]{2,1,0:T(8,128)}, f32[128,128]{1,0:T(8,128)}) custom-call(f32[1024,256]{1,0:T(8,128)} %x_hbm.3, f32[1024,128]{1,0:T(8,128)} %y_hbm.3, s32[4,8]{1,0:T(4,128)} %bitcast.2, s32[2]{0:T(128)} %blocks_hbm.1), custom_call_target="tpu_custom_call" | custom-call | tf_op jit(solution)/shard_map/exchange/pallas_call | solution.py:544
  31.8 3.2 %update.1 = (f32[1024,256]{1,0:T(8,128)}, f32[1024,128]{1,0:T(8,128)}, f32[128,128]{1,0:T(8,128)}) custom-call(f32[1024,256]{1,0:T(8,128)} %x_hbm.3, f32[1024,128]{1,0:T(8,128)} %y_hbm.3, s32[4,8]{1,0:T(4,128)} %bitcast.3, f32[1024,128]{1,0:T(8,128)} %get-tuple-element.9.c_hbm, f32[8,16,384]{2,1,0:T(8,128)} %get-tuple-element.10.m_hbm, ...), custom_call_target="tpu_custom_call" | custom-call | tf_op jit(solution)/shard_map/update/pallas_call | solution.py:599
